TPU v7x, 256 devices: a whole 4x4x8 slice. The times are simulated.
256 devices in a mesh: pipe: 64 (over y, x, z_lo), tp: 4 (over z_hi, core).
Axes of the slice: x: 4, y: 4, z: 8 (z_hi: 2, z_lo: 4; z = z_hi * 4 + z_lo), core: 2. Of those that a mesh axis runs over, the one named last changes fastest.
Arguments:
- stream_in: bfloat16 [64, 256, 6144], P('pipe', None, 'tp')
- grad_in: bfloat16 [64, 256, 6144], P('pipe', None, 'tp'), may hold values from -6 to 6
- fresh_batch: bfloat16 [256, 6144], P(None, 'tp')
- loss_grad: bfloat16 [256, 6144], P(None, 'tp'), may hold values from -6 to 6
- local_stash: bfloat16 [64, 2, 256, 6144], P('pipe', None, None, 'tp')
- partner_stash: bfloat16 [64, 2, 256, 6144], P('pipe', None, None, 'tp')
- norm_gains: float32 [64, 3, 6144], P('pipe', None, 'tp'), may hold values from 0.25 to 1.75
- stash_plan: int32 [2, 64], replicated, may hold values from 0 to 3, as said below
Outputs:
- fwd_out: bfloat16 [64, 256, 6144], P('pipe', None, 'tp')
- bwd_out: bfloat16 [64, 256, 6144], P('pipe', None, 'tp')
- gain_grad: float32 [64, 3, 6144], P('pipe', None, 'tp')
Inputs may be any that keep to these rules, and one draw needn't show every extreme that they name: `stash_plan`: A value k below 2 names the section's own slot k; a value of 2 or more names slot k - 2 of what its mirror partner keeps for it. Sections below 32 always take a stash kept by their partner, the others always one of their own.
All inputs are finite; a program needn't handle non-finite values.
Results may differ from a plain program's by a relative error of at most 0.0097.
Values may be sent and summed in bfloat16 or wider, within the bound.
No kernel may reach another device: no remote copies, remote signals or barrier semaphores. Data moves between devices by JAX's collectives and lax.ppermute only.
A program may use at most 64 MiB of HBM per device.

v0:
```python
import jax
import jax.numpy as jnp
from jax import lax
from jax.sharding import PartitionSpec as P

D = 6144
HEAD_DIM = 128
TICKS = 2


EPSILON = 1e-05


def from_partner(value, axis, apart):
    mask = 2**apart
    pairs = [(source, source ^ mask) for source in range(lax.axis_size(axis))]
    return lax.ppermute(value, axis, pairs)


def passed_along(shard, axis, by):
    length = lax.axis_size(axis)
    pairs = [(i, i + by) for i in range(length) if 0 <= i + by < length]
    return lax.ppermute(shard, axis, pairs)


def normalize(stream):
    values = stream.astype(jnp.float32)
    middle = lax.psum(jnp.sum(values, axis=-1, keepdims=True), "tp") / D
    center = values - middle
    spread = lax.psum(jnp.sum(center * center, axis=-1, keepdims=True), "tp") / D
    scale_inv = lax.rsqrt(spread + EPSILON)
    return (center * scale_inv, scale_inv)


def projections(normed, gain_rows):
    seq_len = normed.shape[0]
    queries = (normed * gain_rows[0]).astype(jnp.bfloat16).reshape(seq_len, -1, HEAD_DIM)
    key_rows = (normed * gain_rows[1]).astype(jnp.bfloat16).reshape(seq_len, -1, HEAD_DIM)
    value_rows = (normed * gain_rows[2]).astype(jnp.bfloat16).reshape(seq_len, -1, HEAD_DIM)
    return (queries, key_rows, value_rows)


def attention_weights(queries, key_rows):
    seq_len = queries.shape[0]
    scores = jnp.einsum(
        "qhd,khd->hqk", queries, key_rows, preferred_element_type=jnp.float32
    ) * HEAD_DIM ** (-0.5)
    row_ids = lax.broadcasted_iota(jnp.int32, (seq_len, seq_len), 0)
    col_ids = lax.broadcasted_iota(jnp.int32, (seq_len, seq_len), 1)
    scores = jnp.where(col_ids <= row_ids, scores, -1e30)
    row_top = jnp.max(scores, axis=-1, keepdims=True)
    raised = jnp.exp(scores - row_top)
    return raised / jnp.sum(raised, axis=-1, keepdims=True)


def forward(stream, gain_rows):
    normed, scale_inv = normalize(stream)
    queries, key_rows, value_rows = projections(normed, gain_rows)
    weights = attention_weights(queries, key_rows).astype(jnp.bfloat16)
    context = jnp.einsum("hqk,khd->qhd", weights, value_rows, preferred_element_type=jnp.float32)
    return (stream.astype(jnp.float32) + context.reshape(stream.shape[0], -1)).astype(jnp.bfloat16)


def backward(stashed, cotangent, gain_rows):
    seq_len = stashed.shape[0]
    normed, scale_inv = normalize(stashed)
    queries, key_rows, value_rows = projections(normed, gain_rows)
    chances = attention_weights(queries, key_rows)
    weights = chances.astype(jnp.bfloat16)
    cot_heads = cotangent.reshape(seq_len, -1, HEAD_DIM)
    value_grad = jnp.einsum("hqk,qhd->khd", weights, cot_heads, preferred_element_type=jnp.float32)
    prob_grad = jnp.einsum(
        "qhd,khd->hqk", cot_heads, value_rows, preferred_element_type=jnp.float32
    )
    score_grad = (
        chances
        * (prob_grad - jnp.sum(prob_grad * chances, axis=-1, keepdims=True))
        * HEAD_DIM ** (-0.5)
    )
    score_grad = score_grad.astype(jnp.bfloat16)
    query_grad = jnp.einsum(
        "hqk,khd->qhd", score_grad, key_rows, preferred_element_type=jnp.float32
    ).reshape(seq_len, -1)
    key_grad = jnp.einsum(
        "hqk,qhd->khd", score_grad, queries, preferred_element_type=jnp.float32
    ).reshape(seq_len, -1)
    value_grad = value_grad.reshape(seq_len, -1)
    normed_grad = query_grad * gain_rows[0] + key_grad * gain_rows[1] + value_grad * gain_rows[2]
    gain_terms = jnp.stack(
        [
            jnp.sum(query_grad * normed, axis=0),
            jnp.sum(key_grad * normed, axis=0),
            jnp.sum(value_grad * normed, axis=0),
        ]
    )
    grad_totals, cross_totals = lax.psum(
        (
            jnp.sum(normed_grad, axis=-1, keepdims=True),
            jnp.sum(normed_grad * normed, axis=-1, keepdims=True),
        ),
        "tp",
    )
    input_grad = scale_inv * (normed_grad - grad_totals / D - normed * (cross_totals / D))
    return ((cotangent.astype(jnp.float32) + input_grad).astype(jnp.bfloat16), gain_terms)


def mirror(payload):
    bit_levels = lax.axis_size("pipe").bit_length() - 1
    for bit_level in range(bit_levels):
        payload = from_partner(payload, "pipe", bit_level)
    return payload


def per_device(
    stream_in, grad_in, fresh_batch, loss_grad, local_stash, partner_stash, norm_gains, stash_plan
):
    sections = lax.axis_size("pipe")
    section = lax.axis_index("pipe")
    slot_count = local_stash.shape[1]
    gain_rows = norm_gains[0]
    stream = stream_in[0]
    cotangent = grad_in[0]
    gain_total = jnp.zeros(gain_rows.shape, jnp.float32)
    held_rows = partner_stash[0]
    for tick_index in range(TICKS):
        if tick_index > 0:
            arrived = passed_along(produced, "pipe", 1)
            stream = jnp.where(section == 0, fresh_batch, arrived)
            came_back = passed_along(returned, "pipe", -1)
            cotangent = jnp.where(section == sections - 1, loss_grad, came_back)
        plan_row = stash_plan[tick_index]
        wanted = lax.dynamic_index_in_dim(plan_row, section, 0, keepdims=False)
        fetched = lax.dynamic_index_in_dim(
            mirror(held_rows), jnp.clip(wanted - slot_count, 0, slot_count - 1), 0, keepdims=False
        )
        own_rows = lax.dynamic_index_in_dim(
            local_stash[0], jnp.clip(wanted, 0, slot_count - 1), 0, keepdims=False
        )
        stashed = jnp.where(wanted < slot_count, own_rows, fetched)
        produced = forward(stream, gain_rows)
        returned, gain_terms = backward(stashed, cotangent, gain_rows)
        gain_total = gain_total + gain_terms
    return (produced[None], returned[None], gain_total[None])


def solution(mesh):
    placed = (
        P("pipe", None, "tp"),
        P("pipe", None, "tp"),
        P(None, "tp"),
        P(None, "tp"),
        P("pipe", None, None, "tp"),
        P("pipe", None, None, "tp"),
        P("pipe", None, "tp"),
        P(),
    )
    return jax.shard_map(
        per_device,
        mesh=mesh,
        in_specs=placed,
        out_specs=(P("pipe", None, "tp"), P("pipe", None, "tp"), P("pipe", None, "tp")),
        check_vma=False,
    )
```

profile of v0, /device:TPU:36, one launch (start us, length us, event | category | flops | bytes accessed | tf_op | source)
XLA Modules:
  0.0 411.2 jit_solution(2456334106366943220)
XLA Ops:
  0.8 36.2 %collective-permute-done.1 = bf16[2,256,1536]{2,1,0:T(8,128)(2,1)S(1)} collective-permute-done((bf16[2,256,1536]{2,1,0:T(8,128)(2,1)}, bf16[2,256,1536]{2,1,0:T(8,128)(2,1)S(1)}, u32[]{:S(2)}, u32[]{:S(2)}) %collective-permute-start.1) | collective-permute-done | bytes 1572896 | tf_op jit(solution)/shard_map/ppermute | solution.py:17
  37.1 3.3 collective-permute-start.2
  40.3 66.4 %collective-permute-done.2 = bf16[2,256,1536]{2,1,0:T(8,128)(2,1)S(1)} collective-permute-done((bf16[2,256,1536]{2,1,0:T(8,128)(2,1)S(1)}, bf16[2,256,1536]{2,1,0:T(8,128)(2,1)S(1)}, u32[]{:S(2)}, u32[]{:S(2)}) %collective-permute-start.2) | collective-permute-done | bytes 1572896 | tf_op jit(solution)/shard_map/ppermute | solution.py:17
  107.9 35.1 %collective-permute-done.3 = bf16[2,256,1536]{2,1,0:T(8,128)(2,1)S(1)} collective-permute-done((bf16[2,256,1536]{2,1,0:T(8,128)(2,1)S(1)}, bf16[2,256,1536]{2,1,0:T(8,128)(2,1)S(1)}, u32[]{:S(2)}, u32[]{:S(2)}) %collective-permute-start.3) | collective-permute-done | bytes 1572896 | tf_op jit(solution)/shard_map/ppermute | solution.py:17
  143.6 36.5 %collective-permute-done.4 = bf16[2,256,1536]{2,1,0:T(8,128)(2,1)S(1)} collective-permute-done((bf16[2,256,1536]{2,1,0:T(8,128)(2,1)S(1)}, bf16[2,256,1536]{2,1,0:T(8,128)(2,1)S(1)}, u32[]{:S(2)}, u32[]{:S(2)}) %collective-permute-start.4) | collective-permute-done | bytes 1572896 | tf_op jit(solution)/shard_map/ppermute | solution.py:17
  181.6 33.1 %collective-permute-done.5 = bf16[2,256,1536]{2,1,0:T(8,128)(2,1)} collective-permute-done((bf16[2,256,1536]{2,1,0:T(8,128)(2,1)S(1)}, bf16[2,256,1536]{2,1,0:T(8,128)(2,1)}, u32[]{:S(2)}, u32[]{:S(2)}) %collective-permute-start.5) | collective-permute-done | bytes 1572896 | tf_op jit(solution)/shard_map/ppermute | solution.py:17
  214.7 3.2 collective-permute-start.6
  231.5 19.3 %collective-permute-done.6 = bf16[2,256,1536]{2,1,0:T(8,128)(2,1)} collective-permute-done((bf16[2,256,1536]{2,1,0:T(8,128)(2,1)}, bf16[2,256,1536]{2,1,0:T(8,128)(2,1)}, u32[]{:S(2)}, u32[]{:S(2)}) %collective-permute-start.6) | collective-permute-done | bytes 1572896 | tf_op jit(solution)/shard_map/ppermute | solution.py:17
  256.1 9.7 %all-reduce.3 = (f32[256,1]{0,1:T(1,128)S(1)}, f32[256,1]{0,1:T(1,128)S(1)}) all-reduce(f32[256,1]{0,1:T(1,128)S(1)} %bitcast.270, f32[256,1]{0,1:T(1,128)S(1)} %bitcast.271), channel_id=1, replica_groups=mesh['pipe'=64,'tp'=4] {'tp'}, use_global_device_ids=true, to_apply=%region_1.2 | all-reduce | flops 512 | bytes 4096 | tf_op jit(solution)/shard_map/psum | solution.py:28
  268.3 12.3 %all-reduce.2 = (f32[256,1]{0,1:T(1,128)S(1)}, f32[256,1]{0,1:T(1,128)S(1)}, f32[256,1]{0,1:T(1,128)S(1)}) all-reduce(f32[256,1]{0,1:T(1,128)S(1)} %bitcast.264, f32[256,1]{0,1:T(1,128)S(1)} %bitcast.265, f32[256,1]{0,1:T(1,128)S(1)} %bitcast.266), channel_id=1, replica_groups=mesh['pipe'=64,'tp'=4] {'tp'}, use_global_device_ids=true, to_apply=%region_3.4 | all-reduce | flops 768 | bytes 6144 | tf_op jit(solution)/shard_map/psum | solution.py:30
  281.9 3.7 fusion.91
  289.1 7.0 %fusion.88 = f32[12,128,256]{2,1,0:T(8,128)} fusion(f32[12,256,256]{2,1,0:T(8,128)} %fusion.91, bf16[256,12,128]{0,2,1:T(8,128)(2,1)S(1)} %broadcast_select_fusion.1, f32[256]{0:T(256)S(1)} %bitcast.252, f32[256]{0:T(256)S(1)} %bitcast.240, f32[12,128]{1,0:T(8,128)S(1)} %bitcast.219, f32[12,256,256]{1,2,0:T(8,128)} %get-tuple-element.54, ...), kind=kOutput, calls=%fused_computation.139 | convolution fusion | flops 208801024 | bytes 8671232 | tf_op jit(solution)/shard_map/hqk,qhd->khd/dot_general | solution.py:84
  296.1 7.1 %fusion.89 = f32[12,128,256]{2,1,0:T(8,128)} fusion(f32[12,256,256]{2,1,0:T(8,128)} %fusion.91, bf16[256,12,128]{0,2,1:T(8,128)(2,1)S(1)} %broadcast_select_fusion.1, f32[256]{0:T(256)S(1)} %bitcast.253, f32[256]{0:T(256)S(1)} %bitcast.241, f32[12,128]{1,0:T(8,128)S(1)} %bitcast.212, f32[12,256,256]{1,2,0:T(8,128)} %get-tuple-element.54, ...), kind=kOutput, calls=%fused_computation.140 | convolution fusion | flops 208801024 | bytes 8671232 | tf_op jit(solution)/shard_map/hqk,khd->qhd/dot_general | solution.py:81
  313.6 13.2 %collective-permute-done = bf16[256,1536]{0,1:T(8,128)(2,1)} collective-permute-done((bf16[256,1536]{0,1:T(8,128)(2,1)}, bf16[256,1536]{0,1:T(8,128)(2,1)}, u32[]{:S(2)}, u32[]{:S(2)}) %collective-permute-start) | collective-permute-done | bytes 786464 | tf_op jit(solution)/shard_map/ppermute | solution.py:23
  328.2 10.0 %all-reduce.1 = (f32[256,1]{0,1:T(1,128)S(1)}, f32[256,1]{0,1:T(1,128)S(1)}, f32[256,1]{0,1:T(1,128)S(1)}, f32[256,1]{0,1:T(1,128)S(1)}) all-reduce(f32[256,1]{0,1:T(1,128)S(1)} %bitcast.273, f32[256,1]{0,1:T(1,128)S(1)} %bitcast.279, f32[256,1]{0,1:T(1,128)S(1)} %bitcast.278, ...), channel_id=1, replica_groups=mesh['pipe'=64,'tp'=4] {'tp'}, use_global_device_ids=true, to_apply=%region_7.8 | all-reduce | flops 1024 | bytes 8192 | tf_op jit(solution)/shard_map/psum | solution.py:28
  338.2 3.1 fusion.46
  341.4 8.1 %collective-permute-start.7 = (bf16[256,1536]{0,1:T(8,128)(2,1)S(1)}, bf16[256,1536]{0,1:T(8,128)(2,1)S(1)}, u32[]{:S(2)}, u32[]{:S(2)}) collective-permute-start(bf16[256,1536]{0,1:T(8,128)(2,1)S(1)} %fusion.46), channel_id=1, source_target_pairs={{4,0},{8,4},{12,8},{16,12},{20,16},{24,20},{28,24},{32,28},{36,32}... | collective-permute-start | bytes 2359304 | tf_op jit(solution)/shard_map/ppermute | solution.py:23
  353.3 10.7 %collective-permute-done.7 = bf16[256,1536]{0,1:T(8,128)(2,1)S(1)} collective-permute-done((bf16[256,1536]{0,1:T(8,128)(2,1)S(1)}, bf16[256,1536]{0,1:T(8,128)(2,1)S(1)}, u32[]{:S(2)}, u32[]{:S(2)}) %collective-permute-start.7) | collective-permute-done | bytes 786464 | tf_op jit(solution)/shard_map/ppermute | solution.py:23
  366.7 7.0 %fusion.17 = f32[12,128,256]{2,1,0:T(8,128)} fusion(f32[12,256,256]{1,2,0:T(8,128)} %fusion.92, bf16[256,12,128]{0,2,1:T(8,128)(2,1)S(1)} %broadcast_select_fusion, f32[256]{0:T(256)S(1)} %bitcast.246, f32[256]{0:T(256)S(1)} %bitcast.233, f32[12,128]{1,0:T(8,128)S(1)} %bitcast.223, f32[12,256,256]{1,2,0:T(8,128)} %get-tuple-element.58, ...), kind=kOutput, calls=%fused_computation.31 | convolution fusion | flops 208801024 | bytes 8671232 | tf_op jit(solution)/shard_map/hqk,qhd->khd/dot_general | solution.py:84
  373.7 7.1 %fusion.20 = f32[12,128,256]{2,1,0:T(8,128)} fusion(f32[12,256,256]{1,2,0:T(8,128)} %fusion.92, bf16[256,12,128]{0,2,1:T(8,128)(2,1)S(1)} %broadcast_select_fusion, f32[256]{0:T(256)S(1)} %bitcast.247, f32[256]{0:T(256)S(1)} %bitcast.234, f32[12,128]{1,0:T(8,128)S(1)} %bitcast.216, f32[12,256,256]{1,2,0:T(8,128)} %get-tuple-element.58, ...), kind=kOutput, calls=%fused_computation.32 | convolution fusion | flops 208801024 | bytes 8671232 | tf_op jit(solution)/shard_map/hqk,khd->qhd/dot_general | solution.py:81
  380.8 3.9 fusion.56
  385.9 11.5 %all-reduce = (f32[256,1]{0,1:T(1,128)S(1)}, f32[256,1]{0,1:T(1,128)S(1)}, f32[256,1]{0,1:T(1,128)S(1)}) all-reduce(f32[256,1]{0,1:T(1,128)S(1)} %bitcast.263, f32[256,1]{0,1:T(1,128)S(1)} %bitcast.275, f32[256,1]{0,1:T(1,128)S(1)} %bitcast.274), channel_id=1, replica_groups=mesh['pipe'=64,'tp'=4] {'tp'}, use_global_device_ids=true, to_apply=%region_9.10 | all-reduce | flops 768 | bytes 6144 | tf_op jit(solution)/shard_map/psum | solution.py:30
  397.4 4.0 fusion.33
  401.4 4.3 %fusion.134 = (f32[12,256]{1,0:T(8,128)S(1)}, f32[12,256,256]{1,2,0:T(8,128)}) fusion(pred[256,256]{0,1:T(8,128)(4,1)S(1)} %iota_compare_fusion, bf16[256,12,128]{0,2,1:T(8,128)(2,1)} %bitcast.210, bf16[256,12,128]{0,2,1:T(8,128)(2,1)} %bitcast.209), kind=kOutput, calls=%fused_computation.214 | convolution fusion | flops 204472576 | bytes 4796416 | tf_op jit(solution)/shard_map/sub | solution.py:52
  (103 shorter events, 50.6 us)
Async XLA Ops:
  0.6 223.3 %copy-start.15 = (bf16[1,256,1536]{2,1,0:T(8,128)(2,1)S(1)}, bf16[1,256,1536]{2,1,0:T(8,128)(2,1)}, u32[]{:S(2)}) copy-start(bf16[1,256,1536]{2,1,0:T(8,128)(2,1)} %param.8) | copy-start | bytes 2359300
  0.6 36.4 %collective-permute-start.1 = (bf16[2,256,1536]{2,1,0:T(8,128)(2,1)}, bf16[2,256,1536]{2,1,0:T(8,128)(2,1)S(1)}, u32[]{:S(2)}, u32[]{:S(2)}) collective-permute-start(bf16[2,256,1536]{2,1,0:T(8,128)(2,1)} %bitcast.280), channel_id=1, source_target_pairs={{0,4},{4,0},{8,12},{12,8},{16,20},{20,16},{24,28},{28,24},{32,36},... | collective-permute-start | bytes 4718600 | tf_op jit(solution)/shard_map/ppermute | solution.py:17
  37.1 69.7 %collective-permute-start.2 = (bf16[2,256,1536]{2,1,0:T(8,128)(2,1)S(1)}, bf16[2,256,1536]{2,1,0:T(8,128)(2,1)S(1)}, u32[]{:S(2)}, u32[]{:S(2)}) collective-permute-start(bf16[2,256,1536]{2,1,0:T(8,128)(2,1)S(1)} %collective-permute-done.1), channel_id=1, source_target_pairs={{0,8},{4,12},{8,0},{12,4},{16,24},{20,28},{24,16},{28,20},{32,40},... | collective-permute-start | bytes 4718600 | tf_op jit(solution)/shard_map/ppermute | solution.py:17
  106.8 36.3 %collective-permute-start.3 = (bf16[2,256,1536]{2,1,0:T(8,128)(2,1)S(1)}, bf16[2,256,1536]{2,1,0:T(8,128)(2,1)S(1)}, u32[]{:S(2)}, u32[]{:S(2)}) collective-permute-start(bf16[2,256,1536]{2,1,0:T(8,128)(2,1)S(1)} %collective-permute-done.2), channel_id=1, source_target_pairs={{0,16},{4,20},{8,24},{12,28},{16,0},{20,4},{24,8},{28,12},{32,48},... | collective-permute-start | bytes 4718600 | tf_op jit(solution)/shard_map/ppermute | solution.py:17
  143.1 37.0 %collective-permute-start.4 = (bf16[2,256,1536]{2,1,0:T(8,128)(2,1)S(1)}, bf16[2,256,1536]{2,1,0:T(8,128)(2,1)S(1)}, u32[]{:S(2)}, u32[]{:S(2)}) collective-permute-start(bf16[2,256,1536]{2,1,0:T(8,128)(2,1)S(1)} %collective-permute-done.3), channel_id=1, source_target_pairs={{0,32},{4,36},{8,40},{12,44},{16,48},{20,52},{24,56},{28,60},{32,0... | collective-permute-start | bytes 4718600 | tf_op jit(solution)/shard_map/ppermute | solution.py:17
  180.0 34.7 %collective-permute-start.5 = (bf16[2,256,1536]{2,1,0:T(8,128)(2,1)S(1)}, bf16[2,256,1536]{2,1,0:T(8,128)(2,1)}, u32[]{:S(2)}, u32[]{:S(2)}) collective-permute-start(bf16[2,256,1536]{2,1,0:T(8,128)(2,1)S(1)} %collective-permute-done.4), channel_id=1, source_target_pairs={{0,64},{4,68},{8,72},{12,76},{16,80},{20,84},{24,88},{28,92},{32,9... | collective-permute-start | bytes 4718600 | tf_op jit(solution)/shard_map/ppermute | solution.py:17
  214.7 36.2 %collective-permute-start.6 = (bf16[2,256,1536]{2,1,0:T(8,128)(2,1)}, bf16[2,256,1536]{2,1,0:T(8,128)(2,1)}, u32[]{:S(2)}, u32[]{:S(2)}) collective-permute-start(bf16[2,256,1536]{2,1,0:T(8,128)(2,1)} %collective-permute-done.5), channel_id=1, source_target_pairs={{0,128},{4,132},{8,136},{12,140},{16,144},{20,148},{24,152},{28,15... | collective-permute-start | bytes 4718600 | tf_op jit(solution)/shard_map/ppermute | solution.py:17
  227.3 27.5 %copy-start.1 = (bf16[1,1,256,1536]{2,3,1,0:T(8,128)(2,1)}, bf16[1,1,256,1536]{2,3,1,0:T(8,128)(2,1)S(1)}, u32[]{:S(2)}) copy-start(bf16[1,1,256,1536]{2,3,1,0:T(8,128)(2,1)S(1)} %copy.56) | copy-start | bytes 2359300
  227.6 2.4 copy-start.16
  227.6 3.6 copy-start.17
  254.9 11.1 %copy-start.2 = (bf16[1,256,1536]{1,2,0:T(8,128)(2,1)}, bf16[1,256,1536]{1,2,0:T(8,128)(2,1)S(1)}, u32[]{:S(2)}) copy-start(bf16[1,256,1536]{1,2,0:T(8,128)(2,1)S(1)} %copy.57) | copy-start | bytes 2359300
  256.1 11.4 %copy-start.3 = (bf16[256,1536]{0,1:T(8,128)(2,1)S(1)}, bf16[256,1536]{0,1:T(8,128)(2,1)}, u32[]{:S(2)}) copy-start(bf16[256,1536]{0,1:T(8,128)(2,1)} %get-tuple-element.36) | copy-start | bytes 2359300
  305.2 4.5 %copy-start.7 = (f32[12,128,256]{2,1,0:T(8,128)S(1)}, f32[12,128,256]{2,1,0:T(8,128)}, u32[]{:S(2)}) copy-start(f32[12,128,256]{2,1,0:T(8,128)} %fusion.89) | copy-start | bytes 4718596
  305.2 4.5 %copy-start.18 = (f32[12,256,256]{1,2,0:T(8,128)S(1)}, f32[12,256,256]{1,2,0:T(8,128)}, u32[]{:S(2)}) copy-start(f32[12,256,256]{1,2,0:T(8,128)} %get-tuple-element.54) | copy-start | bytes 9437188
  305.8 3.9 copy-start.5
  305.8 3.9 copy-start.6
  306.9 19.8 %collective-permute-start = (bf16[256,1536]{0,1:T(8,128)(2,1)}, bf16[256,1536]{0,1:T(8,128)(2,1)}, u32[]{:S(2)}, u32[]{:S(2)}) collective-permute-start(bf16[256,1536]{0,1:T(8,128)(2,1)} %fusion.54), channel_id=1, source_target_pairs={{0,4},{4,8},{8,12},{12,16},{16,20},{20,24},{24,28},{28,32},{32,36}... | collective-permute-start | bytes 2359304 | tf_op jit(solution)/shard_map/ppermute | solution.py:23
  312.1 14.7 %copy-start.13 = (bf16[256,1536]{0,1:T(8,128)(2,1)S(1)}, bf16[256,1536]{0,1:T(8,128)(2,1)}, u32[]{:S(2)}) copy-start(bf16[256,1536]{0,1:T(8,128)(2,1)} %copy.51) | copy-start | bytes 2359300
  313.6 24.6 %copy-start.4 = (bf16[256,1536]{0,1:T(8,128)(2,1)S(1)}, bf16[256,1536]{0,1:T(8,128)(2,1)}, u32[]{:S(2)}) copy-start(bf16[256,1536]{0,1:T(8,128)(2,1)} %get-tuple-element.36) | copy-start | bytes 2359300
  341.4 22.7 %collective-permute-start.7 = (bf16[256,1536]{0,1:T(8,128)(2,1)S(1)}, bf16[256,1536]{0,1:T(8,128)(2,1)S(1)}, u32[]{:S(2)}, u32[]{:S(2)}) collective-permute-start(bf16[256,1536]{0,1:T(8,128)(2,1)S(1)} %fusion.46), channel_id=1, source_target_pairs={{4,0},{8,4},{12,8},{16,12},{20,16},{24,20},{28,24},{32,28},{36,32}... | collective-permute-start | bytes 2359304 | tf_op jit(solution)/shard_map/ppermute | solution.py:23
  350.7 13.4 %copy-start.12 = (bf16[256,1536]{0,1:T(8,128)(2,1)S(1)}, bf16[256,1536]{0,1:T(8,128)(2,1)}, u32[]{:S(2)}) copy-start(bf16[256,1536]{0,1:T(8,128)(2,1)} %copy.68) | copy-start | bytes 2359300
  380.8 3.9 copy-start.9
  380.8 3.9 copy-start.10
  401.4 4.3 %copy-start.14 = (bf16[256,1536]{0,1:T(8,128)(2,1)S(1)}, bf16[256,1536]{0,1:T(8,128)(2,1)}, u32[]{:S(2)}) copy-start(bf16[256,1536]{0,1:T(8,128)(2,1)} %get-tuple-element.42) | copy-start | bytes 2359300
  (3 other events, 3.2 us)
where the time goes:
time: 415 us; the launch traced here: 411 us
  waiting for transfers between devices  251 us (60%)
  matrix products  49.5 us (12%)
  blocking collectives  43.5 us (10%)
  other arithmetic  24.5 us (6%)
  starting transfers between devices  20.8 us (5%)
  local copies, waits for them, and re-layouts  17.6 us (4%)
  between operations  4.75 us (1%)
    ppermute x6, waiting for transfers between devices, from_partner(): return lax.ppermute(value, axis, pairs)  227 us
    ppermute x2, waiting for transfers between devices, passed_along(): return lax.ppermute(shard, axis, pairs)  23.9 us
    psum x2, blocking collectives, normalize(): lax.psum(jnp.sum(center * center, axis=-1, keepdims=True), 'tp') / D  23.8 us
    psum x2, blocking collectives, normalize(): middle = lax.psum(jnp.sum(values, axis=-1, keepdims=True), 'tp') / D  19.7 us
    dot_general x2, matrix products, backward(): jnp.einsum('hqk,khd->qhd', score_grad, key_rows, preferred_element_type=j...  14.2 us
    dot_general x2, matrix products, backward(): jnp.einsum('hqk,qhd->khd', score_grad, queries, preferred_element_type=jn...  14 us
    ppermute x2, starting transfers between devices, passed_along(): return lax.ppermute(shard, axis, pairs)  10.9 us
    ppermute x6, starting transfers between devices, from_partner(): return lax.ppermute(value, axis, pairs)  9.94 us
  transfers between devices with their start and end apart: 8, of which 8 were waited for; matrix products, arithmetic and copies ran while one was open for 4% of the time, Pallas kernels for 0%

commit v1 on v0

v1 whole, which is shorter than its diff:
```python
import jax
import jax.numpy as jnp
from jax import lax
from jax.experimental import pallas as pl
from jax.experimental.pallas import tpu as pltpu

HEAD_DIM = 128
BLOCK = 128
D = 6144
EPSILON = 1e-05
SCALE = HEAD_DIM ** (-0.5)
HEADS_PER_STEP = 2
VMEM_LIMIT = 40 * 1024 * 1024
F32 = jnp.float32
BF16 = jnp.bfloat16


def dot(a, b, dims):
    return lax.dot_general(a, b, (dims, ((), ())), preferred_element_type=F32)


def to_rows(columns):
    tokens = columns[0].shape[0]
    lane = lax.broadcasted_iota(jnp.int32, (tokens, 128), 1)
    wide = jnp.zeros((tokens, 128), F32)
    for i, column in enumerate(columns):
        wide = jnp.where(lane == i, column, wide)
    return wide.T[:8]


def to_columns(rows):
    filler = jnp.zeros((120, rows.shape[1]), F32)
    return jnp.concatenate([rows, filler], axis=0).T


def moments(values):
    total = jnp.sum(values, axis=-1, keepdims=True)
    center = values - total * (1.0 / values.shape[-1])
    return total, jnp.sum(center * center, axis=-1, keepdims=True)


def causal(s):
    rows, cols = s.shape
    row = lax.broadcasted_iota(jnp.int32, s.shape, 0) + (cols - rows)
    col = lax.broadcasted_iota(jnp.int32, s.shape, 1)
    return jnp.where(col <= row, s, -1e30)


def softmax_rows(q, k):
    s = causal(dot(q, k, ((1,), (1,))) * SCALE)
    raised = jnp.exp(s - jnp.max(s, axis=-1, keepdims=True))
    return raised * (1.0 / jnp.sum(raised, axis=-1, keepdims=True))


def pick_kernel(slots, kept, own, stream, sent, stats):
    columns = []
    picked = kept[0, 0]
    sent[...] = picked
    columns += moments(picked.astype(F32))
    columns += moments(own[0, 0].astype(F32))
    columns += moments(stream[...].astype(F32))
    stats[...] = to_rows(columns)


def pick(slots, kept, own, stream):
    tokens, width = stream.shape
    one = (1, 1, tokens, width)
    return pl.pallas_call(
        pick_kernel,
        grid_spec=pltpu.PrefetchScalarGridSpec(
            num_scalar_prefetch=1,
            grid=(1,),
            in_specs=[
                pl.BlockSpec(one, lambda i, slots: (0, slots[0], 0, 0)),
                pl.BlockSpec(one, lambda i, slots: (0, slots[1], 0, 0)),
                pl.BlockSpec((tokens, width), lambda i, slots: (0, 0)),
            ],
            out_specs=[
                pl.BlockSpec((tokens, width), lambda i, slots: (0, 0)),
                pl.BlockSpec((8, tokens), lambda i, slots: (0, 0)),
            ],
        ),
        out_shape=[
            jax.ShapeDtypeStruct((tokens, width), BF16),
            jax.ShapeDtypeStruct((8, tokens), F32),
        ],
        compiler_params=pltpu.CompilerParams(vmem_limit_bytes=VMEM_LIMIT),
        name="pick",
    )(slots, kept, own, stream)


def head_slice(h):
    return pl.ds(pl.multiple_of(h * HEAD_DIM, HEAD_DIM), HEAD_DIM)


def forward_kernel(flag, a_ref, b_ref, gains, norms, out, stats):
    use_b = flag[0] != 0
    tokens, width = out.shape
    cols = to_columns(norms[...])
    mean = jnp.where(use_b, cols[:, 2:3], cols[:, 0:1])
    rstd = jnp.where(use_b, cols[:, 3:4], cols[:, 1:2])

    def head(h):
        at = head_slice(h)
        x = jnp.where(use_b, b_ref[:, at], a_ref[:, at]).astype(F32)
        n = (x - mean) * rstd
        q = (n * gains[0:1, at]).astype(BF16)
        k = (n * gains[1:2, at]).astype(BF16)
        v = (n * gains[2:3, at]).astype(BF16)
        total = jnp.zeros((tokens, 1), F32)
        for lo in range(0, tokens, BLOCK):
            hi = lo + BLOCK
            w = softmax_rows(q[lo:hi], k[:hi]).astype(BF16)
            context = dot(w, v[:hi], ((1,), (0,)))
            out[lo:hi, at] = (x[lo:hi] + context).astype(BF16)

    def step(i, carry):
        for j in range(HEADS_PER_STEP):
            head(i * HEADS_PER_STEP + j)
        return carry

    lax.fori_loop(0, width // HEAD_DIM // HEADS_PER_STEP, step, 0)
    stats[...] = to_rows(moments(out[...].astype(F32)))


SMEM = pl.BlockSpec(memory_space=pltpu.SMEM)
VMEM = pl.BlockSpec(memory_space=pltpu.VMEM)


def forward(flag, a, b, gains, norms):
    tokens, width = a.shape
    heads = width // HEAD_DIM
    return pl.pallas_call(
        forward_kernel,
        in_specs=[SMEM, VMEM, VMEM, VMEM, VMEM],
        out_specs=[VMEM, VMEM],
        out_shape=[
            jax.ShapeDtypeStruct((tokens, width), BF16),
            jax.ShapeDtypeStruct((8, tokens), F32),
        ],
        compiler_params=pltpu.CompilerParams(vmem_limit_bytes=VMEM_LIMIT),
        cost_estimate=pl.CostEstimate(
            flops=4 * heads * tokens * tokens * HEAD_DIM * 8, bytes_accessed=6 * tokens * width, transcendentals=heads * tokens * tokens
        ),
        name="forward",
    )(flag, a, b, gains, norms)


def backward_kernel(flags, za, zb, ea, eb, gains, norms, before, dn_out, h_out, sums, cross_acc, plain_acc):
    use_zb = flags[0] != 0
    use_eb = flags[1] != 0
    tokens, width = dn_out.shape
    cols = to_columns(norms[...])
    mean = jnp.where(use_zb, cols[:, 2:3], cols[:, 0:1])
    rstd = jnp.where(use_zb, cols[:, 3:4], cols[:, 1:2])
    cross_acc[...] = jnp.zeros_like(cross_acc)
    plain_acc[...] = jnp.zeros_like(plain_acc)

    def head(h):
        at = head_slice(h)
        z = jnp.where(use_zb, zb[:, at], za[:, at]).astype(F32)
        e = jnp.where(use_eb, eb[:, at], ea[:, at])
        n = (z - mean) * rstd
        g0, g1, g2 = gains[0:1, at], gains[1:2, at], gains[2:3, at]
        q = (n * g0).astype(BF16)
        k = (n * g1).astype(BF16)
        v = (n * g2).astype(BF16)
        dq, dk, dv = [], None, None
        for lo in range(0, tokens, BLOCK):
            hi = lo + BLOCK
            p = softmax_rows(q[lo:hi], k[:hi])
            w = p.astype(BF16)
            dp = dot(e[lo:hi], v[:hi], ((1,), (1,)))
            row = jnp.sum(dp * p, axis=-1, keepdims=True)
            ds = (p * (dp - row) * SCALE).astype(BF16)
            dq.append(dot(ds, k[:hi], ((1,), (0,))))
            dv_part = dot(w, e[lo:hi], ((0,), (0,)))
            dk_part = dot(ds, q[lo:hi], ((0,), (0,)))
            if dv is not None:
                dv_part = jnp.concatenate([dv + dv_part[:lo], dv_part[lo:]], axis=0)
                dk_part = jnp.concatenate([dk + dk_part[:lo], dk_part[lo:]], axis=0)
            dv, dk = dv_part, dk_part
        dq = jnp.concatenate(dq, axis=0)
        dn = dq * g0 + dk * g1 + dv * g2
        dn_out[:, at] = dn
        plain_acc[...] += dn
        cross_acc[...] += dn * n
        for i, grad in enumerate((dq, dk, dv)):
            h_out[i : i + 1, at] = before[i : i + 1, at] + jnp.sum(grad * n, axis=0, keepdims=True)

    def step(i, carry):
        for j in range(HEADS_PER_STEP):
            head(i * HEADS_PER_STEP + j)
        return carry

    lax.fori_loop(0, width // HEAD_DIM // HEADS_PER_STEP, step, 0)
    sums[...] = to_rows(
        [jnp.sum(plain_acc[...], axis=-1, keepdims=True), jnp.sum(cross_acc[...], axis=-1, keepdims=True)]
    )


def backward(flags, za, zb, ea, eb, gains, norms, before):
    tokens, width = za.shape
    heads = width // HEAD_DIM
    return pl.pallas_call(
        backward_kernel,
        in_specs=[SMEM] + [VMEM] * 7,
        out_specs=[VMEM] * 3,
        out_shape=[
            jax.ShapeDtypeStruct((tokens, width), F32),
            jax.ShapeDtypeStruct((3, width), F32),
            jax.ShapeDtypeStruct((8, tokens), F32),
        ],
        scratch_shapes=[pltpu.VMEM((tokens, HEAD_DIM), F32), pltpu.VMEM((tokens, HEAD_DIM), F32)],
        compiler_params=pltpu.CompilerParams(vmem_limit_bytes=VMEM_LIMIT),
        cost_estimate=pl.CostEstimate(
            flops=14 * heads * tokens * tokens * HEAD_DIM * 8, bytes_accessed=10 * tokens * width, transcendentals=heads * tokens * tokens
        ),
        name="backward",
    )(flags, za, zb, ea, eb, gains, norms, before)


def finish_kernel(flags, za, zb, ea, eb, norms, dn, sums, out):
    use_zb = flags[0] != 0
    use_eb = flags[1] != 0
    cols = to_columns(norms[...])
    mean = jnp.where(use_zb, cols[:, 2:3], cols[:, 0:1])
    rstd = jnp.where(use_zb, cols[:, 3:4], cols[:, 1:2])
    means = to_columns(sums[...])
    plain, cross = means[:, 0:1] * (1.0 / D), means[:, 1:2] * (1.0 / D)

    def step(h, carry):
        at = head_slice(h)
        z = jnp.where(use_zb, zb[:, at], za[:, at]).astype(F32)
        e = jnp.where(use_eb, eb[:, at], ea[:, at]).astype(F32)
        n = (z - mean) * rstd
        out[:, at] = (e + rstd * (dn[:, at] - plain - n * cross)).astype(BF16)
        return carry

    lax.fori_loop(0, out.shape[1] // HEAD_DIM, step, 0)


def finish(flags, za, zb, ea, eb, norms, dn, sums):
    tokens, width = za.shape
    return pl.pallas_call(
        finish_kernel,
        in_specs=[SMEM] + [VMEM] * 7,
        out_specs=VMEM,
        out_shape=jax.ShapeDtypeStruct((tokens, width), BF16),
        compiler_params=pltpu.CompilerParams(vmem_limit_bytes=VMEM_LIMIT),
        name="finish",
    )(flags, za, zb, ea, eb, norms, dn, sums)


def over_tp(rows, combine):
    for mask in (1, 2):
        rows = combine(rows, lax.ppermute(rows, "tp", [(i, i ^ mask) for i in range(4)]))
    return rows


def joined(width):
    count = [width]

    def combine(mine, other):
        a, b = mine.reshape(-1, 2, mine.shape[-1]), other.reshape(-1, 2, mine.shape[-1])
        apart = (a[:, 0] - b[:, 0]) / count[0]
        squares = a[:, 1] + b[:, 1] + apart * apart * (0.5 * count[0])
        count[0] *= 2
        return jnp.stack([a[:, 0] + b[:, 0], squares], axis=1).reshape(mine.shape)

    return combine


def norm_rows(rows):
    pairs = rows.reshape(-1, 2, rows.shape[-1]) / D
    return jnp.stack([pairs[:, 0], lax.rsqrt(pairs[:, 1] + EPSILON)], axis=1).reshape(rows.shape)


def per_device(
    stream_in, grad_in, fresh_batch, loss_grad, local_stash, partner_stash, norm_gains, stash_plan
):
    sections = lax.axis_size("pipe")
    half = sections // 2
    section = lax.axis_index("pipe")
    slots = local_stash.shape[1]
    gains = norm_gains[0]
    stream, cotangent = stream_in[0], grad_in[0]
    width = stream.shape[1]

    to_next = [(i, i + 1) for i in range(sections - 1)]
    to_last = [(i + 1, i) for i in range(sections - 1)]
    mirrored = [(sections - 1 - s, s) for s in range(half)]

    kept_at = jnp.clip(stash_plan[:, sections - 1 - section] - slots, 0, slots - 1)
    own_at = jnp.clip(stash_plan[:, section], 0, slots - 1)
    early = (section < half).astype(jnp.int32)
    first = (section == 0).astype(jnp.int32)
    last = (section == sections - 1).astype(jnp.int32)

    sent0, rows0 = pick(jnp.stack([kept_at[0], own_at[0]]), partner_stash, local_stash, stream)
    z0 = lax.ppermute(sent0, "pipe", mirrored)
    sent1, rows1 = pick(jnp.stack([kept_at[1], own_at[1]]), partner_stash, local_stash, fresh_batch)
    z1 = lax.ppermute(sent1, "pipe", mirrored)
    own0 = lax.dynamic_index_in_dim(local_stash[0], own_at[0], 0, keepdims=False)
    own1 = lax.dynamic_index_in_dim(local_stash[0], own_at[1], 0, keepdims=False)

    norms = norm_rows(over_tp(jnp.concatenate([rows0[:6], rows1[:6]], axis=0), joined(width)))
    got = lax.ppermute(jnp.concatenate([norms[0:2], norms[6:8]], axis=0), "pipe", mirrored)
    fill = jnp.zeros((4, norms.shape[1]), F32)
    norms_z0 = jnp.concatenate([norms[2:4], got[0:2], fill], axis=0)
    norms_z1 = jnp.concatenate([norms[8:10], got[2:4], fill], axis=0)

    produced, out_rows = forward(jnp.zeros((1,), jnp.int32), stream, stream, gains, jnp.concatenate([norms[4:6], norms[4:6], fill]))
    arrived = lax.ppermute(produced, "pipe", to_next)
    flags0 = jnp.stack([early, jnp.zeros_like(early)])
    grad, gain_total, sums = backward(
        flags0, own0, z0, cotangent, cotangent, gains, norms_z0, jnp.zeros((3, width), F32)
    )
    out_norms = norm_rows(over_tp(out_rows[:2], joined(width)))
    out_norms = lax.ppermute(out_norms, "pipe", to_next)
    sums = over_tp(sums, lambda a, b: a + b)
    returned = finish(flags0, own0, z0, cotangent, cotangent, norms_z0, grad, sums)
    came_back = lax.ppermute(returned, "pipe", to_last)

    fwd_out, _ = forward(
        jnp.stack([first]), arrived, fresh_batch, gains, jnp.concatenate([out_norms, norms[10:12], fill])
    )
    flags1 = jnp.stack([early, last])
    grad, gain_total, sums = backward(flags1, own1, z1, came_back, loss_grad, gains, norms_z1, gain_total)
    sums = over_tp(sums, lambda a, b: a + b)
    bwd_out = finish(flags1, own1, z1, came_back, loss_grad, norms_z1, grad, sums)
    return (fwd_out[None], bwd_out[None], gain_total[None])


def solution(mesh):
    from jax.sharding import PartitionSpec as P

    placed = (
        P("pipe", None, "tp"),
        P("pipe", None, "tp"),
        P(None, "tp"),
        P(None, "tp"),
        P("pipe", None, None, "tp"),
        P("pipe", None, None, "tp"),
        P("pipe", None, "tp"),
        P(),
    )
    return jax.shard_map(
        per_device,
        mesh=mesh,
        in_specs=placed,
        out_specs=(P("pipe", None, "tp"), P("pipe", None, "tp"), P("pipe", None, "tp")),
        check_vma=False,
    )
```

time: 415 us -> 196 us (0.47)
  the two profiles are of different devices: /device:TPU:36 before, /device:TPU:49 now
where the time goes in v1:
time: 196 us; the launch traced here: 195 us
  waiting for transfers between devices  76.7 us (39%)
  Pallas kernels  59.6 us (30%)
  starting transfers between devices  38.2 us (19%)
  local copies, waits for them, and re-layouts  12.2 us (6%)
  between operations  4.53 us (2%)
  other arithmetic  3.9 us (2%)
    ppermute x1, waiting for transfers between devices, per_device(): z1 = lax.ppermute(sent1, 'pipe', mirrored)  32.1 us
    pallas_call x2, Pallas kernels, backward(): pl.pallas_call(backward_kernel, in_specs=[SMEM] + [VMEM] * 7, out_specs=[...  26.7 us
    ppermute x8, waiting for transfers between devices, over_tp(): lax.ppermute(rows, 'tp', [(i, i ^ mask) for i in range(4)])  25.4 us
    pallas_call x2, Pallas kernels, forward(): pl.pallas_call(forward_kernel, in_specs=[SMEM, VMEM, VMEM, VMEM, VMEM], o...  18.7 us
    ppermute x1, waiting for transfers between devices, per_device(): came_back = lax.ppermute(returned, 'pipe', to_last)  18.5 us
    ppermute x8, starting transfers between devices, over_tp(): lax.ppermute(rows, 'tp', [(i, i ^ mask) for i in range(4)])  15.2 us
    unnamed x40, local copies, waits for them, and re-layouts  10.9 us
    pallas_call x2, Pallas kernels, finish(): pl.pallas_call(finish_kernel, in_specs=[SMEM] + [VMEM] * 7, out_specs=VME...  9.74 us
  transfers between devices with their start and end apart: 14, of which 9 were waited for; matrix products, arithmetic and copies ran while one was open for 1% of the time, Pallas kernels for 19%

profile of v1, /device:TPU:49, one launch (start us, length us, event | category | flops | bytes accessed | tf_op | source)
XLA Modules:
  0.0 195.1 jit_solution(429584479639564916)
XLA Ops:
  2.5 2.6 %pad_add_fusion = (s32[2]{0:T(128)S(1)}, s32[2]{0:T(128)S(1)}) fusion(s32[1]{0:T(128)} %bitcast.3, s32[1]{0:T(128)} %bitcast.2, s32[1]{0:T(128)} %bitcast.5, s32[1]{0:T(128)} %bitcast.4), kind=kLoop, calls=%fused_computation.54 | loop fusion | flops 4 | bytes 32 | tf_op jit(solution)/shard_map/stack | solution.py:300
  5.1 1.4 copy-done
  6.5 1.4 copy-done.2
  9.0 2.2 %pick.2 = (bf16[256,1536]{1,0:T(8,128)(2,1)}, f32[8,256]{1,0:T(8,128)S(1)}) custom-call(s32[2]{0:T(128)S(1)} %get-tuple-element.65.slots, bf16[1,2,256,1536]{3,2,1,0:T(8,128)(2,1)S(1)} %copy-done.2, bf16[1,2,256,1536]{3,2,1,0:T(8,128)(2,1)S(1)} %copy-done, bf16[256,1536]{1,0:T(8,128)(2,1)S(1)} %bitcast.47), custom_call_target="tpu_custom_call" | custom-call | tf_op jit(solution)/shard_map/pick/pallas_call | solution.py:68
  11.3 2.2 %pick.3 = (bf16[256,1536]{1,0:T(8,128)(2,1)}, f32[8,256]{1,0:T(8,128)S(1)}) custom-call(s32[2]{0:T(128)S(1)} %get-tuple-element.66.slots, bf16[1,2,256,1536]{3,2,1,0:T(8,128)(2,1)S(1)} %copy-done.3, bf16[1,2,256,1536]{3,2,1,0:T(8,128)(2,1)S(1)} %copy-done.1, bf16[256,1536]{1,0:T(8,128)(2,1)S(1)} %copy-done.7), custom_call_target="tpu_custom_call" | custom-call | tf_op jit(solution)/shard_map/pick/pallas_call | solution.py:68
  14.2 6.5 %collective-permute-start.7 = (bf16[256,1536]{1,0:T(8,128)(2,1)}, bf16[256,1536]{1,0:T(8,128)(2,1)}, u32[]{:S(2)}, u32[]{:S(2)}) collective-permute-start(bf16[256,1536]{1,0:T(8,128)(2,1)} %get-tuple-element.22), channel_id=1, source_target_pairs={{252,0},{248,4},{244,8},{240,12},{236,16},{232,20},{228,24},{224,2... | collective-permute-start | bytes 2359304 | tf_op jit(solution)/shard_map/ppermute | solution.py:301
  24.5 5.2 %collective-permute-start.1 = (f32[12,256]{1,0:T(8,128)S(1)}, f32[12,256]{1,0:T(8,128)S(1)}, u32[]{:S(2)}, u32[]{:S(2)}) collective-permute-start(f32[12,256]{1,0:T(8,128)S(1)} %reshape.132), channel_id=1, source_target_pairs={{0,2},{1,3},{2,0},{3,1},{4,6},{5,7},{6,4},{7,5},{8,10},{9,11},{10,... | collective-permute-start | bytes 36872 | tf_op jit(solution)/shard_map/ppermute | solution.py:257
  29.9 14.1 %collective-permute-done.1 = f32[12,256]{1,0:T(8,128)S(1)} collective-permute-done((f32[12,256]{1,0:T(8,128)S(1)}, f32[12,256]{1,0:T(8,128)S(1)}, u32[]{:S(2)}, u32[]{:S(2)}) %collective-permute-start.1) | collective-permute-done | bytes 12320 | tf_op jit(solution)/shard_map/ppermute | solution.py:257
  45.3 8.4 %forward.2 = (bf16[256,1536]{1,0:T(8,128)(2,1)S(1)}, f32[8,256]{1,0:T(8,128)S(1)}) custom-call(s32[1]{0:T(128)} %constant.21.clone.1.flag, bf16[256,1536]{1,0:T(8,128)(2,1)S(1)} %bitcast.48, bf16[256,1536]{1,0:T(8,128)(2,1)S(1)} %bitcast.49, f32[3,1536]{1,0:T(4,128)S(1)} %bitcast.50, f32[8,256]{1,0:T(8,128)S(1)} %maximum_maximum_fusion.norms), custom_call_target="tpu_custom_call" | custom-call | flops 3221225472 | bytes 2359296 | tf_op jit(solution)/shard_map/forward/pallas_call | solution.py:133
  56.8 4.7 %collective-permute-done.4 = f32[2,256]{1,0:T(2,128)S(1)} collective-permute-done((f32[2,256]{1,0:T(2,128)S(1)}, f32[2,256]{1,0:T(2,128)S(1)}, u32[]{:S(2)}, u32[]{:S(2)}) %collective-permute-start.4) | collective-permute-done | bytes 2080 | tf_op jit(solution)/shard_map/ppermute | solution.py:257
  61.6 4.5 %collective-permute-start.5 = (f32[2,256]{1,0:T(2,128)S(1)}, f32[2,256]{1,0:T(2,128)S(1)}, u32[]{:S(2)}, u32[]{:S(2)}) collective-permute-start(f32[2,256]{1,0:T(2,128)S(1)} %maximum_bitcast_fusion.1), channel_id=1, source_target_pairs={{0,4},{4,8},{8,12},{12,16},{16,20},{20,24},{24,28},{28,32},{32,36}... | collective-permute-start | bytes 6152 | tf_op jit(solution)/shard_map/ppermute | solution.py:320
  66.9 13.7 %backward.2 = (f32[256,1536]{1,0:T(8,128)S(1)}, f32[3,1536]{1,0:T(4,128)S(1)}, f32[8,256]{1,0:T(8,128)S(1)}) custom-call(s32[2]{0:T(128)S(1)} %pad_add_fusion.3.flags, bf16[256,1536]{1,0:T(8,128)(2,1)S(1)} %get-tuple-element.32.za, bf16[256,1536]{1,0:T(8,128)(2,1)} %collective-permute-done.7.zb, bf16[256,1536]{1,0:T(8,128)(2,1)S(1)} %bitcast.43, ...), custom_call_target="tpu_custom_call" | custom-call | flops 11274289152 | bytes 3932160 | tf_op jit(solution)/shard_map/backward/pallas_call | solution.py:205
  80.6 2.4 %collective-permute-start.9 = (f32[8,256]{1,0:T(8,128)S(1)}, f32[8,256]{1,0:T(8,128)S(1)}, u32[]{:S(2)}, u32[]{:S(2)}) collective-permute-start(f32[8,256]{1,0:T(8,128)S(1)} %get-tuple-element.24), channel_id=1, source_target_pairs={{0,1},{1,0},{2,3},{3,2},{4,5},{5,4},{6,7},{7,6},{8,9},{9,8},{10,11... | collective-permute-start | bytes 24584 | tf_op jit(solution)/shard_map/ppermute | solution.py:257
  84.9 1.3 collective-permute-start.6
  86.2 4.1 %collective-permute-done.10 = f32[8,256]{1,0:T(8,128)S(1)} collective-permute-done((f32[8,256]{1,0:T(8,128)S(1)}, f32[8,256]{1,0:T(8,128)S(1)}, u32[]{:S(2)}, u32[]{:S(2)}) %collective-permute-start.10) | collective-permute-done | bytes 8224 | tf_op jit(solution)/shard_map/ppermute | solution.py:257
  90.3 5.2 %finish.2 = bf16[256,1536]{1,0:T(8,128)(2,1)} custom-call(s32[2]{0:T(128)S(1)} %pad_add_fusion.3.flags, bf16[256,1536]{1,0:T(8,128)(2,1)S(1)} %get-tuple-element.32.za, bf16[256,1536]{1,0:T(8,128)(2,1)} %collective-permute-done.7.zb, bf16[256,1536]{1,0:T(8,128)(2,1)S(1)} %bitcast.45, bf16[256,1536]{1,0:T(8,128)(2,1)S(1)} %bitcast.46, ...), custom_call_target="tpu_custom_call" | custom-call | tf_op jit(solution)/shard_map/finish/pallas_call | solution.py:245
  95.5 7.5 %collective-permute-start.11 = (bf16[256,1536]{1,0:T(8,128)(2,1)}, bf16[256,1536]{1,0:T(8,128)(2,1)S(1)}, u32[]{:S(2)}, u32[]{:S(2)}) collective-permute-start(bf16[256,1536]{1,0:T(8,128)(2,1)} %finish.2), channel_id=1, source_target_pairs={{4,0},{8,4},{12,8},{16,12},{20,16},{24,20},{28,24},{32,28},{36,32}... | collective-permute-start | bytes 2359304 | tf_op jit(solution)/shard_map/ppermute | solution.py:323
  103.1 1.9 collective-permute-start.2
  105.0 32.1 %collective-permute-done.6.zb = bf16[256,1536]{1,0:T(8,128)(2,1)S(1)} collective-permute-done((bf16[256,1536]{1,0:T(8,128)(2,1)}, bf16[256,1536]{1,0:T(8,128)(2,1)S(1)}, u32[]{:S(2)}, u32[]{:S(2)}) %collective-permute-start.6) | collective-permute-done | bytes 786464 | tf_op jit(solution)/shard_map/ppermute | solution.py:303
  138.0 18.5 %collective-permute-done.11.ea = bf16[256,1536]{1,0:T(8,128)(2,1)S(1)} collective-permute-done((bf16[256,1536]{1,0:T(8,128)(2,1)}, bf16[256,1536]{1,0:T(8,128)(2,1)S(1)}, u32[]{:S(2)}, u32[]{:S(2)}) %collective-permute-start.11) | collective-permute-done | bytes 786464 | tf_op jit(solution)/shard_map/ppermute | solution.py:323
  160.8 13.0 %backward.3 = (f32[256,1536]{1,0:T(8,128)S(1)}, f32[3,1536]{1,0:T(4,128)S(1)}, f32[8,256]{1,0:T(8,128)S(1)}) custom-call(s32[2]{0:T(128)S(1)} %pad_add_fusion.2.flags, bf16[256,1536]{1,0:T(8,128)(2,1)S(1)} %get-tuple-element.33.za, bf16[256,1536]{1,0:T(8,128)(2,1)S(1)} %copy-done.12, bf16[256,1536]{1,0:T(8,128)(2,1)S(1)} %copy-done.15, ...), custom_call_target="tpu_custom_call" | custom-call | flops 11274289152 | bytes 3932160 | tf_op jit(solution)/shard_map/backward/pallas_call | solution.py:205
  176.0 3.6 %collective-permute-start.13 = (f32[8,256]{1,0:T(8,128)S(1)}, f32[8,256]{1,0:T(8,128)S(1)}, u32[]{:S(2)}, u32[]{:S(2)}) collective-permute-start(f32[8,256]{1,0:T(8,128)S(1)} %add.138), channel_id=1, source_target_pairs={{0,2},{1,3},{2,0},{3,1},{4,6},{5,7},{6,4},{7,5},{8,10},{9,11},{10,... | collective-permute-start | bytes 24584 | tf_op jit(solution)/shard_map/ppermute | solution.py:257
  179.6 10.3 %forward.3 = (bf16[256,1536]{1,0:T(8,128)(2,1)}, f32[8,256]{1,0:T(8,128)}) custom-call(s32[1]{0:T(128)} %bitcast.flag, bf16[256,1536]{1,0:T(8,128)(2,1)} %collective-permute-done.2.a_ref, bf16[256,1536]{1,0:T(8,128)(2,1)S(1)} %copy-done.8, f32[3,1536]{1,0:T(4,128)S(1)} %bitcast.53, f32[8,256]{1,0:T(8,128)S(1)} %get-tuple-element.63.norms), custom_call_target="tpu_custom_call" | custom-call | flops 3221225472 | bytes 2359296 | tf_op jit(solution)/shard_map/forward/pallas_call | solution.py:133
  190.6 4.6 %finish.3 = bf16[256,1536]{1,0:T(8,128)(2,1)} custom-call(s32[2]{0:T(128)S(1)} %pad_add_fusion.2.flags, bf16[256,1536]{1,0:T(8,128)(2,1)S(1)} %get-tuple-element.33.za, bf16[256,1536]{1,0:T(8,128)(2,1)S(1)} %copy-done.13, bf16[256,1536]{1,0:T(8,128)(2,1)S(1)} %copy-done.16, bf16[256,1536]{1,0:T(8,128)(2,1)S(1)} %copy-done.10, ...), custom_call_target="tpu_custom_call" | custom-call | tf_op jit(solution)/shard_map/finish/pallas_call | solution.py:245
  (88 shorter events, 19.1 us)
Async XLA Ops:
  9.0 2.2 %copy-start.1 = (bf16[1,2,256,1536]{3,2,1,0:T(8,128)(2,1)S(1)}, bf16[1,2,256,1536]{3,2,1,0:T(8,128)(2,1)}, u32[]{:S(2)}) copy-start(bf16[1,2,256,1536]{3,2,1,0:T(8,128)(2,1)} %own.3) | copy-start | bytes 4718596
  9.0 2.2 %copy-start.3 = (bf16[1,2,256,1536]{3,2,1,0:T(8,128)(2,1)S(1)}, bf16[1,2,256,1536]{3,2,1,0:T(8,128)(2,1)}, u32[]{:S(2)}) copy-start(bf16[1,2,256,1536]{3,2,1,0:T(8,128)(2,1)} %kept.3) | copy-start | bytes 4718596
  9.0 2.2 %copy-start.7 = (bf16[256,1536]{1,0:T(8,128)(2,1)S(1)}, bf16[256,1536]{1,0:T(8,128)(2,1)}, u32[]{:S(2)}) copy-start(bf16[256,1536]{1,0:T(8,128)(2,1)} %b_ref.1) | copy-start | bytes 2359300
  13.5 10.8 %collective-permute-start = (f32[12,256]{1,0:T(8,128)S(1)}, f32[12,256]{1,0:T(8,128)S(1)}, u32[]{:S(2)}, u32[]{:S(2)}) collective-permute-start(f32[12,256]{1,0:T(8,128)S(1)} %pad_maximum_fusion), channel_id=1, source_target_pairs={{0,1},{1,0},{2,3},{3,2},{4,5},{5,4},{6,7},{7,6},{8,9},{9,8},{10,11... | collective-permute-start | bytes 36872 | tf_op jit(solution)/shard_map/ppermute | solution.py:257
  14.2 52.7 %collective-permute-start.7 = (bf16[256,1536]{1,0:T(8,128)(2,1)}, bf16[256,1536]{1,0:T(8,128)(2,1)}, u32[]{:S(2)}, u32[]{:S(2)}) collective-permute-start(bf16[256,1536]{1,0:T(8,128)(2,1)} %get-tuple-element.22), channel_id=1, source_target_pairs={{252,0},{248,4},{244,8},{240,12},{236,16},{232,20},{228,24},{224,2... | collective-permute-start | bytes 2359304 | tf_op jit(solution)/shard_map/ppermute | solution.py:301
  24.5 5.3 %copy-start.18 = (f32[1,3,1536]{2,0,1:T(1,128)S(1)}, f32[1,3,1536]{2,0,1:T(1,128)}, u32[]{:S(2)}) copy-start(f32[1,3,1536]{2,0,1:T(1,128)} %param.14) | copy-start | bytes 55300
  24.5 19.6 %collective-permute-start.1 = (f32[12,256]{1,0:T(8,128)S(1)}, f32[12,256]{1,0:T(8,128)S(1)}, u32[]{:S(2)}, u32[]{:S(2)}) collective-permute-start(f32[12,256]{1,0:T(8,128)S(1)} %reshape.132), channel_id=1, source_target_pairs={{0,2},{1,3},{2,0},{3,1},{4,6},{5,7},{6,4},{7,5},{8,10},{9,11},{10,... | collective-permute-start | bytes 36872 | tf_op jit(solution)/shard_map/ppermute | solution.py:257
  45.3 21.5 %copy-start.4 = (bf16[1,256,1536]{2,1,0:T(8,128)(2,1)S(1)}, bf16[1,256,1536]{2,1,0:T(8,128)(2,1)}, u32[]{:S(2)}) copy-start(bf16[1,256,1536]{2,1,0:T(8,128)(2,1)} %param.9) | copy-start | bytes 2359300
  53.7 13.1 %copy-start.17 = (bf16[256,1536]{1,0:T(8,128)(2,1)}, bf16[256,1536]{1,0:T(8,128)(2,1)S(1)}, u32[]{:S(2)}) copy-start(bf16[256,1536]{1,0:T(8,128)(2,1)S(1)} %get-tuple-element.18) | copy-start | bytes 2359300
  53.8 1.4 collective-permute-start.3
  55.1 6.4 %collective-permute-start.4 = (f32[2,256]{1,0:T(2,128)S(1)}, f32[2,256]{1,0:T(2,128)S(1)}, u32[]{:S(2)}, u32[]{:S(2)}) collective-permute-start(f32[2,256]{1,0:T(2,128)S(1)} %maximum_bitcast_fusion), channel_id=1, source_target_pairs={{0,2},{1,3},{2,0},{3,1},{4,6},{5,7},{6,4},{7,5},{8,10},{9,11},{10,... | collective-permute-start | bytes 6152 | tf_op jit(solution)/shard_map/ppermute | solution.py:257
  55.6 10.5 %collective-permute-start.8 = (f32[4,256]{1,0:T(4,128)S(1)}, f32[4,256]{1,0:T(4,128)S(1)}, u32[]{:S(2)}, u32[]{:S(2)}) collective-permute-start(f32[4,256]{1,0:T(4,128)S(1)} %pad_maximum_fusion.2), channel_id=1, source_target_pairs={{252,0},{248,4},{244,8},{240,12},{236,16},{232,20},{228,24},{224,2... | collective-permute-start | bytes 12296 | tf_op jit(solution)/shard_map/ppermute | solution.py:308
  61.6 5.2 %collective-permute-start.5 = (f32[2,256]{1,0:T(2,128)S(1)}, f32[2,256]{1,0:T(2,128)S(1)}, u32[]{:S(2)}, u32[]{:S(2)}) collective-permute-start(f32[2,256]{1,0:T(2,128)S(1)} %maximum_bitcast_fusion.1), channel_id=1, source_target_pairs={{0,4},{4,8},{8,12},{12,16},{16,20},{20,24},{24,28},{28,32},{32,36}... | collective-permute-start | bytes 6152 | tf_op jit(solution)/shard_map/ppermute | solution.py:320
  80.6 3.2 %collective-permute-start.9 = (f32[8,256]{1,0:T(8,128)S(1)}, f32[8,256]{1,0:T(8,128)S(1)}, u32[]{:S(2)}, u32[]{:S(2)}) collective-permute-start(f32[8,256]{1,0:T(8,128)S(1)} %get-tuple-element.24), channel_id=1, source_target_pairs={{0,1},{1,0},{2,3},{3,2},{4,5},{5,4},{6,7},{7,6},{8,9},{9,8},{10,11... | collective-permute-start | bytes 24584 | tf_op jit(solution)/shard_map/ppermute | solution.py:257
  83.8 6.5 %collective-permute-start.10 = (f32[8,256]{1,0:T(8,128)S(1)}, f32[8,256]{1,0:T(8,128)S(1)}, u32[]{:S(2)}, u32[]{:S(2)}) collective-permute-start(f32[8,256]{1,0:T(8,128)S(1)} %add.136), channel_id=1, source_target_pairs={{0,2},{1,3},{2,0},{3,1},{4,6},{5,7},{6,4},{7,5},{8,10},{9,11},{10,... | collective-permute-start | bytes 24584 | tf_op jit(solution)/shard_map/ppermute | solution.py:257
  84.9 52.2 %collective-permute-start.6 = (bf16[256,1536]{1,0:T(8,128)(2,1)}, bf16[256,1536]{1,0:T(8,128)(2,1)S(1)}, u32[]{:S(2)}, u32[]{:S(2)}) collective-permute-start(bf16[256,1536]{1,0:T(8,128)(2,1)} %get-tuple-element.21), channel_id=1, source_target_pairs={{252,0},{248,4},{244,8},{240,12},{236,16},{232,20},{228,24},{224,2... | collective-permute-start | bytes 2359304 | tf_op jit(solution)/shard_map/ppermute | solution.py:303
  95.5 61.1 %collective-permute-start.11 = (bf16[256,1536]{1,0:T(8,128)(2,1)}, bf16[256,1536]{1,0:T(8,128)(2,1)S(1)}, u32[]{:S(2)}, u32[]{:S(2)}) collective-permute-start(bf16[256,1536]{1,0:T(8,128)(2,1)} %finish.2), channel_id=1, source_target_pairs={{4,0},{8,4},{12,8},{16,12},{20,16},{24,20},{28,24},{32,28},{36,32}... | collective-permute-start | bytes 2359304 | tf_op jit(solution)/shard_map/ppermute | solution.py:323
  103.1 76.5 %collective-permute-start.2 = (bf16[256,1536]{1,0:T(8,128)(2,1)}, bf16[256,1536]{1,0:T(8,128)(2,1)}, u32[]{:S(2)}, u32[]{:S(2)}) collective-permute-start(bf16[256,1536]{1,0:T(8,128)(2,1)} %copy-done.17), channel_id=1, source_target_pairs={{0,4},{4,8},{8,12},{12,16},{16,20},{20,24},{24,28},{28,32},{32,36}... | collective-permute-start | bytes 2359304 | tf_op jit(solution)/shard_map/ppermute | solution.py:314
  160.8 18.8 %copy-start.8 = (bf16[256,1536]{1,0:T(8,128)(2,1)S(1)}, bf16[256,1536]{1,0:T(8,128)(2,1)}, u32[]{:S(2)}) copy-start(bf16[256,1536]{1,0:T(8,128)(2,1)} %b_ref.1) | copy-start | bytes 2359300
  173.9 2.1 %collective-permute-start.12 = (f32[8,256]{1,0:T(8,128)S(1)}, f32[8,256]{1,0:T(8,128)S(1)}, u32[]{:S(2)}, u32[]{:S(2)}) collective-permute-start(f32[8,256]{1,0:T(8,128)S(1)} %get-tuple-element.27), channel_id=1, source_target_pairs={{0,1},{1,0},{2,3},{3,2},{4,5},{5,4},{6,7},{7,6},{8,9},{9,8},{10,11... | collective-permute-start | bytes 24584 | tf_op jit(solution)/shard_map/ppermute | solution.py:257
  176.0 14.5 %collective-permute-start.13 = (f32[8,256]{1,0:T(8,128)S(1)}, f32[8,256]{1,0:T(8,128)S(1)}, u32[]{:S(2)}, u32[]{:S(2)}) collective-permute-start(f32[8,256]{1,0:T(8,128)S(1)} %add.138), channel_id=1, source_target_pairs={{0,2},{1,3},{2,0},{3,1},{4,6},{5,7},{6,4},{7,5},{8,10},{9,11},{10,... | collective-permute-start | bytes 24584 | tf_op jit(solution)/shard_map/ppermute | solution.py:257
  179.6 10.9 %copy-start.10 = (bf16[256,1536]{1,0:T(8,128)(2,1)S(1)}, bf16[256,1536]{1,0:T(8,128)(2,1)}, u32[]{:S(2)}) copy-start(bf16[256,1536]{1,0:T(8,128)(2,1)} %eb.3) | copy-start | bytes 2359300
  179.6 10.9 %copy-start.13 = (bf16[256,1536]{1,0:T(8,128)(2,1)S(1)}, bf16[256,1536]{1,0:T(8,128)(2,1)}, u32[]{:S(2)}) copy-start(bf16[256,1536]{1,0:T(8,128)(2,1)} %copy-done.11) | copy-start | bytes 2359300
  179.6 10.9 %copy-start.16 = (bf16[256,1536]{1,0:T(8,128)(2,1)S(1)}, bf16[256,1536]{1,0:T(8,128)(2,1)}, u32[]{:S(2)}) copy-start(bf16[256,1536]{1,0:T(8,128)(2,1)} %copy-done.14) | copy-start | bytes 2359300
  (9 other events, 10.3 us)

commit v2 on v0

v2 whole, which is shorter than its diff:
```python
import jax
import jax.numpy as jnp
from jax import lax
from jax.experimental import pallas as pl
from jax.experimental.pallas import tpu as pltpu
from jax.sharding import PartitionSpec as P

HEAD_DIM = 128
BLOCK = 128
D = 6144
PARTS = 4
EPSILON = 1e-05
SCALE = HEAD_DIM ** (-0.5)
EXP2_SCALE = SCALE * 1.4426950408889634
HEADS_PER_STEP = 6
DIRECT_HEADS = 4
F32 = jnp.float32
BF16 = jnp.bfloat16
SMEM = pl.BlockSpec(memory_space=pltpu.SMEM)
VMEM = pl.BlockSpec(memory_space=pltpu.VMEM)
HBM = pl.BlockSpec(memory_space=pltpu.HBM)
PARAMS = pltpu.CompilerParams(vmem_limit_bytes=16 * 1024 * 1024)
ALL_VMEM = pltpu.CompilerParams(vmem_limit_bytes=56 * 1024 * 1024)


def dot(a, b, dims):
    return lax.dot_general(a, b, (dims, ((), ())), preferred_element_type=F32)


OWN_STASH0, OWN_STASH1, KEPT_STASH0, KEPT_STASH1, STREAM, FRESH = range(6)


def to_rows(columns):
    tokens = next(c for c in columns if c is not None).shape[0]
    lane = lax.broadcasted_iota(jnp.int32, (tokens, 128), 1)
    wide = jnp.zeros((tokens, 128), F32)
    for i, column in enumerate(columns):
        if column is not None:
            wide = jnp.where(lane == i, column, wide)
    return wide.T[: max(8, len(columns))]


def statistics_rows(found):
    columns = [None] * 16
    for place, (total, squares) in found.items():
        columns[place], columns[place + 8] = total, squares
    return to_rows(columns)


def spread(row):
    return jnp.broadcast_to(row, (HEAD_DIM, row.shape[1])).T


def moments(values):
    total = jnp.sum(values, axis=-1, keepdims=True)
    center = values - total * (1.0 / values.shape[-1])
    return total, jnp.sum(center * center, axis=-1, keepdims=True)


def joined_pair(sums, squares, other_sums, other_squares, count):
    apart = sums - other_sums
    return sums + other_sums, squares + other_squares + apart * apart * (0.5 / count)


def join_statistics(a, b, count):
    return jnp.concatenate(joined_pair(a[0:8], a[8:16], b[0:8], b[8:16], count), axis=0)


def join_gradients(a, b, count):
    total, squares = joined_pair(a[2:3], a[3:4], b[2:3], b[3:4], count)
    return jnp.concatenate([a[0:2] + b[0:2], total, squares, a[4:8]], axis=0)


def normalizer(total, squares):
    return total * (1.0 / D), lax.rsqrt(squares * (1.0 / D) + EPSILON)


def half_count(width):
    return width * (PARTS // 2)


def statistics_norm(mine, other, which, width):
    both = join_statistics(mine[...], other[...], half_count(width))
    return normalizer(both[which : which + 1], both[which + 8 : which + 9])


def gradients_norm(mine, other, width):
    both = join_gradients(mine[...], other[...], half_count(width))
    return normalizer(both[2:3], both[3:4])


def slot_of(plan, tick, section, first):
    return jnp.clip(plan[tick, section] - first, 0, 1)


def pick_kernel(plan, kept, own, stream, fresh, sent0, direct, around, own0, own1, rows, buffers, sems):
    section, sections = lax.axis_index("pipe"), plan.shape[1]
    cut = direct.shape[1]
    partner = sections - 1 - section
    copies = [
        pltpu.make_async_copy(kept.at[0, slot_of(plan, 0, partner, 2)], sent0, sems.at[0]),
        pltpu.make_async_copy(kept.at[0, slot_of(plan, 1, partner, 2)], buffers.at[0], sems.at[1]),
        pltpu.make_async_copy(own.at[0, slot_of(plan, 0, section, 0)], own0, sems.at[2]),
        pltpu.make_async_copy(own.at[0, slot_of(plan, 1, section, 0)], own1, sems.at[3]),
        pltpu.make_async_copy(stream.at[0], buffers.at[1], sems.at[4]),
        pltpu.make_async_copy(fresh, buffers.at[2], sems.at[5]),
    ]
    refs = [sent0, buffers.at[0], own0, own1, buffers.at[1], buffers.at[2]]
    places = (KEPT_STASH0, KEPT_STASH1, OWN_STASH0, OWN_STASH1, STREAM, FRESH)
    for copy in copies:
        copy.start()
    found = {}
    for place, copy, ref in zip(places, copies, refs):
        copy.wait()
        found[place] = moments(ref[...].astype(F32))
    rows[...] = statistics_rows(found)
    direct[...] = buffers[0, :, :cut]
    around[...] = buffers[0, :, cut:]


def pick(plan, kept, own, stream, fresh):
    tokens, width = fresh.shape
    cut = DIRECT_HEADS * HEAD_DIM
    whole = jax.ShapeDtypeStruct((tokens, width), BF16)
    return pl.pallas_call(
        pick_kernel,
        in_specs=[SMEM, HBM, HBM, HBM, HBM],
        out_specs=[VMEM] * 6,
        out_shape=[
            whole,
            jax.ShapeDtypeStruct((tokens, cut), BF16),
            jax.ShapeDtypeStruct((tokens, width - cut), BF16),
            whole,
            whole,
            jax.ShapeDtypeStruct((16, tokens), F32),
        ],
        scratch_shapes=[pltpu.VMEM((3, tokens, width), BF16), pltpu.SemaphoreType.DMA((6,))],
        compiler_params=ALL_VMEM,
        name="pick",
    )(plan, kept, own, stream, fresh)


def head_slice(h):
    return pl.ds(pl.multiple_of(h * HEAD_DIM, HEAD_DIM), HEAD_DIM)


def each_head(heads, body):
    def step(i, carry):
        for j in range(HEADS_PER_STEP):
            body(i * HEADS_PER_STEP + j)
        return carry

    lax.fori_loop(0, heads // HEADS_PER_STEP, step, 0)


def causal(s):
    key = lax.broadcasted_iota(jnp.int32, s.shape, 0)
    query = lax.broadcasted_iota(jnp.int32, s.shape, 1)
    return jnp.where(key <= query, s, -1e30)


def softmax_block(s, lo):
    s = s * EXP2_SCALE
    s = jnp.concatenate([s[:lo], causal(s[lo:])], axis=0) if lo else causal(s)
    raised = jnp.exp2(s - jnp.max(s, axis=0, keepdims=True))
    return raised * (1.0 / jnp.sum(raised, axis=0, keepdims=True))


def padded(block, tokens):
    missing = tokens - block.shape[0]
    return jnp.concatenate([block, jnp.zeros((missing, block.shape[1]), block.dtype)], axis=0) if missing else block


def forward_body(pick, gains, norm, out, mean, rstd):
    tokens, width = out.shape
    mean[...] = spread(norm[0])
    rstd[...] = spread(norm[1])

    def head(h):
        at = head_slice(h)
        x = pick(at).astype(F32)
        n = (x - mean[...]) * rstd[...]
        q = (n * gains[0:1, at]).astype(BF16)
        k = (n * gains[1:2, at]).astype(BF16)
        v = (n * gains[2:3, at]).astype(BF16)
        scores = dot(k, q, ((1,), (1,)))
        w = []
        for lo in range(0, tokens, BLOCK):
            hi = lo + BLOCK
            w.append(padded(softmax_block(scores[:hi, lo:hi], lo).astype(BF16), tokens))
        out[:, at] = (x + dot(jnp.concatenate(w, axis=1), v, ((0,), (0,)))).astype(BF16)

    each_head(width // HEAD_DIM, head)


def forward0_kernel(stream, gains, mine, other, out, rows, mean, rstd):
    norm = statistics_norm(mine, other, STREAM, out.shape[1])
    forward_body(lambda at: stream[:, at], gains, norm, out, mean, rstd)
    total, squares = moments(out[...].astype(F32))
    rows[...] = to_rows([None, None, total, squares])


def forward1_kernel(arrived, fresh, gains, late_mine, late_other, mine, other, out, mean, rstd):
    first = lax.axis_index("pipe") == 0
    width = out.shape[1]
    norm = [
        jnp.where(first, a, b)
        for a, b in zip(statistics_norm(mine, other, FRESH, width), gradients_norm(late_mine, late_other, width))
    ]
    forward_body(lambda at: jnp.where(first, fresh[:, at], arrived[:, at]), gains, norm, out, mean, rstd)


def local_call(kernel, out_shape, scratch, operands, name):
    return pl.pallas_call(
        kernel,
        in_specs=[VMEM] * len(operands),
        out_specs=[VMEM] * len(out_shape),
        out_shape=out_shape,
        scratch_shapes=scratch,
        compiler_params=PARAMS,
        name=name,
    )(*operands)


def forward(kernel, name, with_rows, *operands):
    tokens, width = operands[0].shape
    out_shape = [jax.ShapeDtypeStruct((tokens, width), BF16)]
    if with_rows:
        out_shape.append(jax.ShapeDtypeStruct((8, tokens), F32))
    return local_call(kernel, out_shape, [pltpu.VMEM((tokens, HEAD_DIM), F32)] * 2, operands, name)


def backward_body(pick, pick_gains, norm, before, dn_out, h_out, sums, mean, rstd, plain, cross):
    tokens, width = dn_out.shape
    mean[...] = spread(norm[0])
    rstd[...] = spread(norm[1])
    plain[...] = jnp.zeros_like(plain)
    cross[...] = jnp.zeros_like(cross)

    def head(h):
        at = head_slice(h)
        z, e = pick(h, at)
        n = (z.astype(F32) - mean[...]) * rstd[...]
        g = pick_gains(at)
        g0, g1, g2 = g[0:1], g[1:2], g[2:3]
        q = (n * g0).astype(BF16)
        k = (n * g1).astype(BF16)
        v = (n * g2).astype(BF16)
        scores = dot(k, q, ((1,), (1,)))
        dp = dot(v, e, ((1,), (1,)))
        w, ds = [], []
        for lo in range(0, tokens, BLOCK):
            hi = lo + BLOCK
            p = softmax_block(scores[:hi, lo:hi], lo)
            t = p * dp[:hi, lo:hi]
            w.append(padded(p.astype(BF16), tokens))
            ds.append(padded((t - p * jnp.sum(t, axis=0, keepdims=True)).astype(BF16), tokens))
        w, ds = jnp.concatenate(w, axis=1), jnp.concatenate(ds, axis=1)
        dv = dot(w, e, ((1,), (0,)))
        dk = dot(ds, q, ((1,), (0,)))
        dq = dot(ds, k, ((0,), (0,)))
        dn = dq * (g0 * SCALE) + dk * (g1 * SCALE) + dv * g2
        dn_out[:, at] = dn
        plain[...] += dn
        cross[...] += dn * n
        parts = [jnp.sum(grad * n, axis=0, keepdims=True) for grad in (dq, dk, dv)]
        total = jnp.concatenate([parts[0] * SCALE, parts[1] * SCALE, parts[2]], axis=0)
        h_out[0:3, at] = total if before is None else total + before(at)

    each_head(width // HEAD_DIM, head)
    sums[...] = to_rows([jnp.sum(plain[...], axis=-1, keepdims=True), jnp.sum(cross[...], axis=-1, keepdims=True)])


def finish_body(pick, norm, mine, other, dn, out, mean, rstd, plain, cross):
    means = (mine[0:2] + other[0:2]) * (1.0 / D)
    mean[...] = spread(norm[0])
    rstd[...] = spread(norm[1])
    plain[...] = spread(means[0:1])
    cross[...] = spread(means[1:2])

    def head(h):
        at = head_slice(h)
        z, e = pick(h, at)
        n = (z.astype(F32) - mean[...]) * rstd[...]
        out[:, at] = (e.astype(F32) + rstd[...] * (dn[:, at] - plain[...] - n * cross[...])).astype(BF16)

    each_head(out.shape[1] // HEAD_DIM, head)


def is_early():
    return lax.axis_index("pipe") < lax.axis_size("pipe") // 2


def pick_tick1(own_z, direct_z, around_z, own_e, got_e, loss_e):
    section, sections = lax.axis_index("pipe"), lax.axis_size("pipe")
    early = section < sections // 2
    here = section < sections // 2 - 1
    last = section == sections - 1

    def pick(h, at):
        first = jnp.minimum(h, DIRECT_HEADS - 1)
        second = jnp.maximum(h - DIRECT_HEADS, 0)
        got = jnp.where(h < DIRECT_HEADS, direct_z[:, head_slice(first)], around_z[:, head_slice(second)])
        e = jnp.where(last, loss_e[:, at], jnp.where(here, own_e[:, at], got_e[:, at]))
        return jnp.where(early, got, own_z[:, at]), e

    return pick


def late_backward0_kernel(z, e, gains, mine, other, *rest):
    @pl.when(jnp.logical_not(is_early()))
    def _():
        norm = statistics_norm(mine, other, OWN_STASH0, rest[0].shape[1])
        backward_body(lambda h, at: (z[:, at], e[:, at]), lambda at: gains[:, at], norm, None, *rest)


def early_backward0_kernel(z, e, gains, got_stats, dn, h_out, *rest):
    @pl.when(is_early())
    def _():
        tokens, width = dn.shape
        norm = normalizer(got_stats[0:1], got_stats[2:3])
        backward_body(lambda h, at: (z[:, at], e[:, at]), lambda at: gains[:, at], norm, None, dn, h_out, *rest)
        h_out[3:4, :] = jnp.zeros((1, width), F32)
        h_out[3:4, 0:tokens] = got_stats[1:2]
        h_out[3:4, tokens : 2 * tokens] = got_stats[3:4]


def late_finish0_kernel(z, e, stats_mine, stats_other, mine, other, dn, out, *rest):
    @pl.when(jnp.logical_not(is_early()))
    def _():
        norm = statistics_norm(stats_mine, stats_other, OWN_STASH0, out.shape[1])
        finish_body(lambda h, at: (z[:, at], e[:, at]), norm, mine, other, dn, out, *rest)


def early_finish0_kernel(z, e, got_stats, mine, other, dn, out, *rest):
    @pl.when(is_early())
    def _():
        norm = normalizer(got_stats[0:1], got_stats[2:3])
        finish_body(lambda h, at: (z[:, at], e[:, at]), norm, mine, other, dn, out, *rest)


def tick1_norm(mine, other, got_part, width):
    early, tokens = is_early(), mine.shape[1]
    sent = normalizer(got_part[3:4, 0:tokens], got_part[3:4, tokens : 2 * tokens])
    return [jnp.where(early, a, b) for a, b in zip(sent, statistics_norm(mine, other, OWN_STASH1, width))]


def backward1_kernel(oz, dz, az, oe, ge, le, gains, part, got_part, mine, other, dn, h_out, *rest):
    early = is_early()
    backward_body(
        pick_tick1(oz, dz, az, oe, ge, le),
        lambda at: gains[:, at],
        tick1_norm(mine, other, got_part, dn.shape[1]),
        lambda at: jnp.where(early, got_part[0:3, at], part[0:3, at]),
        dn,
        h_out,
        *rest,
    )


def finish1_kernel(oz, dz, az, oe, ge, le, stats_mine, stats_other, got_part, mine, other, dn, out, *rest):
    norm = tick1_norm(stats_mine, stats_other, got_part, out.shape[1])
    finish_body(pick_tick1(oz, dz, az, oe, ge, le), norm, mine, other, dn, out, *rest)


def backward(kernel, name, gain_rows, *operands):
    tokens, width = operands[0].shape
    out_shape = [
        jax.ShapeDtypeStruct((tokens, width), F32),
        jax.ShapeDtypeStruct((gain_rows, width), F32),
        jax.ShapeDtypeStruct((8, tokens), F32),
    ]
    return local_call(kernel, out_shape, [pltpu.VMEM((tokens, HEAD_DIM), F32)] * 4, operands, name)


def finish(kernel, name, *operands):
    tokens, width = operands[0].shape
    out_shape = [jax.ShapeDtypeStruct((tokens, width), BF16)]
    return local_call(kernel, out_shape, [pltpu.VMEM((tokens, HEAD_DIM), F32)] * 4, operands, name)[0]


def routes(sections):
    half, last = sections // 2, sections - 1
    to_next = [(s, s + 1) for s in range(last)]
    late_back = [(s, s - 1) for s in range(half, sections)]
    early_back = [(s, (s - 1) % half) for s in range(half)]
    early_on = [(s, (s + 1) % half) for s in range(half)]
    stash_ahead = [(last - s, (s - 1) % half) for s in range(half)]
    mirrored = [(last - s, s) for s in range(half)]
    across = [(last - s, s ^ 3) for s in range(half)]
    along = [(s ^ 3, s) for s in range(half)]
    return to_next, late_back, early_back, early_on, stash_ahead, mirrored, across, along


def over_tp(value, mask, sections=None):
    if sections is None:
        return lax.ppermute(value, "tp", [(i, i ^ mask) for i in range(PARTS)])
    pairs = [(s * PARTS + i, s * PARTS + (i ^ mask)) for s in sections for i in range(PARTS)]
    return lax.ppermute(value, ("pipe", "tp"), pairs)


def per_device(
    stream_in, grad_in, fresh_batch, loss_grad, local_stash, partner_stash, norm_gains, stash_plan
):
    gains = norm_gains[0]
    cotangent = grad_in[0]
    width = fresh_batch.shape[1]
    to_next, late_back, early_back, early_on, stash_ahead, mirrored, across, along = routes(lax.axis_size("pipe"))

    def moved(value, pairs):
        return lax.ppermute(value, "pipe", pairs)

    def after(value, *others):
        return lax.optimization_barrier((value,) + others)[0]

    half = lax.axis_size("pipe") // 2
    low, high = range(half), range(half, 2 * half)
    sent0, direct, around, own_z0, own_z1, rows = pick(
        stash_plan, partner_stash, local_stash, stream_in, fresh_batch
    )
    got_z0 = moved(sent0, stash_ahead)
    got_e0 = moved(cotangent, early_back)
    got_gains = moved(gains, early_back)
    stats_mine = join_statistics(rows, over_tp(rows, 1), width)
    late_other = over_tp(stats_mine, 2, high)
    late_stats = (stats_mine, late_other)
    both = join_statistics(*late_stats, half_count(width))
    kept = [both[place : place + 1] for place in (KEPT_STASH0, KEPT_STASH1, KEPT_STASH0 + 8, KEPT_STASH1 + 8)]
    got_stats = moved(jnp.concatenate(kept), stash_ahead)
    stats = (stats_mine, late_other + over_tp(stats_mine, 2, low))

    late_tick0 = (own_z0, cotangent)
    grad, late_part, sums = backward(late_backward0_kernel, "late_backward0", 3, *late_tick0, gains, *late_stats)
    sums_mine = sums + over_tp(sums, 1, high)
    sums_other = over_tp(sums_mine, 2, high)
    produced, out_rows = forward(forward0_kernel, "forward0", True, after(stream_in[0], sums_mine), gains, *stats)
    grad = after(grad, produced)
    late_returned = finish(
        late_finish0_kernel, "late_finish0", *late_tick0, *late_stats, sums_mine, sums_other, grad
    )
    came_back = moved(late_returned, late_back)
    got_out_rows = moved(out_rows, to_next)
    around = moved(after(around, got_stats, late_returned), across)
    got_z1a = moved(after(direct, got_stats, late_returned), mirrored)

    early_tick0 = (got_z0, got_e0)
    grad, early_part, sums = backward(
        early_backward0_kernel, "early_backward0", 4, *early_tick0, got_gains, after(got_stats, late_returned)
    )
    gain_back = moved(early_part, early_on)
    sums_mine = sums + over_tp(sums, 1, low)
    sums_other = over_tp(sums_mine, 2, low)
    grad, around = lax.optimization_barrier((grad, around, gain_back, got_out_rows))[:2]
    early_returned = finish(
        early_finish0_kernel, "early_finish0", *early_tick0, got_stats, sums_mine, sums_other, grad
    )
    got_z1b = moved(around, along)
    arrived = moved(after(produced, early_returned), to_next)

    tick1 = (own_z1, got_z1a, got_z1b, early_returned, came_back, loss_grad)
    grad, gain_total, sums = backward(
        backward1_kernel, "backward1", 3, *tick1, gains, late_part, gain_back, *late_stats
    )
    rows = sums + got_out_rows
    sums_mine = join_gradients(rows, over_tp(rows, 1), width)
    sums1 = (sums_mine, over_tp(sums_mine, 2))
    fwd_out = forward(forward1_kernel, "forward1", False, arrived, fresh_batch, gains, *sums1, *stats)[0]
    bwd_out = finish(finish1_kernel, "finish1", *tick1, *late_stats, gain_back, *sums1, grad)
    return (fwd_out[None], bwd_out[None], gain_total[None])


def solution(mesh):
    placed = (
        P("pipe", None, "tp"),
        P("pipe", None, "tp"),
        P(None, "tp"),
        P(None, "tp"),
        P("pipe", None, None, "tp"),
        P("pipe", None, None, "tp"),
        P("pipe", None, "tp"),
        P(),
    )
    return jax.shard_map(
        per_device,
        mesh=mesh,
        in_specs=placed,
        out_specs=(P("pipe", None, "tp"), P("pipe", None, "tp"), P("pipe", None, "tp")),
        check_vma=False,
    )
```

time: 415 us -> 124 us (0.30)
  the two profiles are of different devices: /device:TPU:36 before, /device:TPU:6 now
where the time goes in v2:
time: 124 us
  starting transfers between devices  51.5 us (42%)
  waiting for transfers between devices  42 us (34%)
  Pallas kernels  26.4 us (21%)
  local copies, waits for them, and re-layouts  1.8 us (1%)
    ppermute x11, starting transfers between devices, moved(): return lax.ppermute(value, 'pipe', pairs)  35.2 us
    pallas_call x8, Pallas kernels, local_call(): pl.pallas_call(kernel, in_specs=[VMEM] * len(operands), out_specs=[VMEM]...  20.4 us
    ppermute x6, waiting for transfers between devices, over_tp(): return lax.ppermute(value, ('pipe', 'tp'), pairs)  18.2 us
    ppermute x6, starting transfers between devices, over_tp(): return lax.ppermute(value, ('pipe', 'tp'), pairs)  13.9 us
    ppermute x11, waiting for transfers between devices, moved(): return lax.ppermute(value, 'pipe', pairs)  12.3 us
    ppermute x3, waiting for transfers between devices, over_tp(): return lax.ppermute(value, 'tp', [(i, i ^ mask) for i in range(PARTS)])  11.5 us
    pallas_call x1, Pallas kernels, pick(): pl.pallas_call(pick_kernel, in_specs=[SMEM, HBM, HBM, HBM, HBM], out_spec...  5.92 us
  transfers between devices with their start and end apart: 20, of which 10 were waited for; matrix products, arithmetic and copies ran while one was open for 1% of the time, Pallas kernels for 14%

profile of v2, /device:TPU:6, one launch (start us, length us, event | category | flops | bytes accessed | tf_op | source)
XLA Modules:
  0.0 123.5 jit_solution(12802730451386330803)
XLA Ops:
  0.7 5.9 %pick.1 = (bf16[256,1536]{1,0:T(8,128)(2,1)}, bf16[256,512]{1,0:T(8,128)(2,1)}, bf16[256,1024]{1,0:T(8,128)(2,1)}, bf16[256,1536]{1,0:T(8,128)(2,1)}, bf16[256,1536]{1,0:T(8,128)(2,1)}, /*index=5*/f32[16,256]{1,0:T(8,128)}) custom-call(s32[2,64]{1,0:T(2,128)} %plan.1, bf16[1,2,256,1536]{3,2,1,0:T(8,128)(2,1)} %kept.1, bf16[1,2,256,1536]{3,2,1,0:T(8,128)(2,1)} %own.1, ...), custom_call_target="tpu_custom_call" | custom-call | tf_op jit(solution)/shard_map/pick/pallas_call | solution.py:125
  6.7 1.4 %collective-permute-done = f32[16,256]{1,0:T(8,128)S(1)} collective-permute-done((f32[16,256]{1,0:T(8,128)}, f32[16,256]{1,0:T(8,128)S(1)}, u32[]{:S(2)}, u32[]{:S(2)}) %collective-permute-start) | collective-permute-done | bytes 16416 | tf_op jit(solution)/shard_map/ppermute | solution.py:397
  9.5 6.8 %collective-permute-start.5 = (bf16[256,1536]{1,0:T(8,128)(2,1)S(1)}, bf16[256,1536]{1,0:T(8,128)(2,1)S(1)}, u32[]{:S(2)}, u32[]{:S(2)}) collective-permute-start(bf16[256,1536]{1,0:T(8,128)(2,1)S(1)} %bitcast.9), channel_id=1, source_target_pairs={{0,124},{4,0},{8,4},{12,8},{16,12},{20,16},{24,20},{28,24},{32,28}... | collective-permute-start | bytes 2359304 | tf_op jit(solution)/shard_map/ppermute | solution.py:411
  16.3 1.3 %collective-permute-start.4 = (bf16[256,1536]{1,0:T(8,128)(2,1)}, bf16[256,1536]{1,0:T(8,128)(2,1)S(1)}, u32[]{:S(2)}, u32[]{:S(2)}) collective-permute-start(bf16[256,1536]{1,0:T(8,128)(2,1)} %get-tuple-element.33), channel_id=1, source_target_pairs={{252,124},{248,0},{244,4},{240,8},{236,12},{232,16},{228,20},{224,... | collective-permute-start | bytes 2359304 | tf_op jit(solution)/shard_map/ppermute | solution.py:411
  17.6 6.4 %collective-permute-start.3 = (f32[16,256]{1,0:T(8,128)S(1)}, f32[16,256]{1,0:T(8,128)S(1)}, u32[]{:S(2)}, u32[]{:S(2)}) collective-permute-start(f32[16,256]{1,0:T(8,128)S(1)} %pad_maximum_fusion.mine.stats_mine), channel_id=1, source_target_pairs={{0,2},{1,3},{2,0},{3,1},{4,6},{5,7},{6,4},{7,5},{8,10},{9,11},{10,... | collective-permute-start | bytes 49160 | tf_op jit(solution)/shard_map/ppermute | solution.py:399
  27.9 11.0 %collective-permute-done.3 = f32[16,256]{1,0:T(8,128)S(1)} collective-permute-done((f32[16,256]{1,0:T(8,128)S(1)}, f32[16,256]{1,0:T(8,128)S(1)}, u32[]{:S(2)}, u32[]{:S(2)}) %collective-permute-start.3) | collective-permute-done | bytes 16416 | tf_op jit(solution)/shard_map/ppermute | solution.py:399
  38.9 2.8 %forward0.1 = (bf16[256,1536]{1,0:T(8,128)(2,1)S(1)}, f32[8,256]{1,0:T(8,128)S(1)}) custom-call(bf16[256,1536]{1,0:T(8,128)(2,1)S(1)} %bitcast.8, f32[3,1536]{1,0:T(4,128)S(1)} %bitcast.13, f32[16,256]{1,0:T(8,128)S(1)} %pad_maximum_fusion.mine.stats_mine, f32[16,256]{1,0:T(8,128)S(1)} %add.46.other), custom_call_target="tpu_custom_call" | custom-call | tf_op jit(solution)/shard_map/forward0/pallas_call | solution.py:214
  41.8 3.1 %collective-permute-done.6.got_stats = f32[4,256]{1,0:T(4,128)S(1)} collective-permute-done((f32[4,256]{1,0:T(4,128)S(1)}, f32[4,256]{1,0:T(4,128)S(1)}, u32[]{:S(2)}, u32[]{:S(2)}) %collective-permute-start.6) | collective-permute-done | bytes 4128 | tf_op jit(solution)/shard_map/ppermute | solution.py:411
  46.8 1.9 %collective-permute-start.7 = (f32[3,1536]{1,0:T(4,128)S(1)}, f32[3,1536]{1,0:T(4,128)S(1)}, u32[]{:S(2)}, u32[]{:S(2)}) collective-permute-start(f32[3,1536]{1,0:T(4,128)S(1)} %bitcast.14), channel_id=1, source_target_pairs={{0,124},{4,0},{8,4},{12,8},{16,12},{20,16},{24,20},{28,24},{32,28}... | collective-permute-start | bytes 55304 | tf_op jit(solution)/shard_map/ppermute | solution.py:411
  48.8 3.8 %collective-permute-done.7.gains = f32[3,1536]{1,0:T(4,128)S(1)} collective-permute-done((f32[3,1536]{1,0:T(4,128)S(1)}, f32[3,1536]{1,0:T(4,128)S(1)}, u32[]{:S(2)}, u32[]{:S(2)}) %collective-permute-start.7) | collective-permute-done | bytes 18464 | tf_op jit(solution)/shard_map/ppermute | solution.py:411
  52.6 5.2 %early_backward0.1 = (f32[256,1536]{1,0:T(8,128)S(1)}, f32[4,1536]{1,0:T(4,128)S(1)}, f32[8,256]{1,0:T(8,128)S(1)}) custom-call(bf16[256,1536]{1,0:T(8,128)(2,1)S(1)} %collective-permute-done.4.z, bf16[256,1536]{1,0:T(8,128)(2,1)S(1)} %collective-permute-done.5.e, f32[3,1536]{1,0:T(4,128)S(1)} %collective-permute-done.7.gains, ...), custom_call_target="tpu_custom_call" | custom-call | tf_op jit(solution)/shard_map/early_backward0/pallas_call | solution.py:214
  57.8 1.9 %collective-permute-start.12 = (f32[4,1536]{1,0:T(4,128)S(1)}, f32[4,1536]{1,0:T(4,128)S(1)}, u32[]{:S(2)}, u32[]{:S(2)}) collective-permute-start(f32[4,1536]{1,0:T(4,128)S(1)} %get-tuple-element.41), channel_id=1, source_target_pairs={{0,4},{4,8},{8,12},{12,16},{16,20},{20,24},{24,28},{28,32},{32,36}... | collective-permute-start | bytes 73736 | tf_op jit(solution)/shard_map/ppermute | solution.py:411
  59.7 2.9 %collective-permute-start.13 = (f32[8,256]{1,0:T(8,128)S(1)}, f32[8,256]{1,0:T(8,128)S(1)}, u32[]{:S(2)}, u32[]{:S(2)}) collective-permute-start(f32[8,256]{1,0:T(8,128)S(1)} %get-tuple-element.42), channel_id=1, source_target_pairs={{0,4},{4,8},{8,12},{12,16},{16,20},{20,24},{24,28},{28,32},{32,36}... | collective-permute-start | bytes 24584 | tf_op jit(solution)/shard_map/ppermute | solution.py:411
  62.7 5.3 %collective-permute-done.13 = f32[8,256]{1,0:T(8,128)S(1)} collective-permute-done((f32[8,256]{1,0:T(8,128)S(1)}, f32[8,256]{1,0:T(8,128)S(1)}, u32[]{:S(2)}, u32[]{:S(2)}) %collective-permute-start.13) | collective-permute-done | bytes 8224 | tf_op jit(solution)/shard_map/ppermute | solution.py:411
  68.0 13.6 %collective-permute-start.16 = (bf16[256,1024]{1,0:T(8,128)(2,1)S(1)}, bf16[256,1024]{1,0:T(8,128)(2,1)S(1)}, u32[]{:S(2)}, u32[]{:S(2)}) collective-permute-start(bf16[256,1024]{1,0:T(8,128)(2,1)S(1)} %collective-permute-done.11), channel_id=1, source_target_pairs={{12,0},{8,4},{4,8},{0,12},{28,16},{24,20},{20,24},{16,28},{44,32},... | collective-permute-start | bytes 1572872 | tf_op jit(solution)/shard_map/ppermute | solution.py:411
  82.9 1.9 %collective-permute-start.9 = (f32[8,256]{1,0:T(8,128)S(1)}, f32[8,256]{1,0:T(8,128)S(1)}, u32[]{:S(2)}, u32[]{:S(2)}) collective-permute-start(f32[8,256]{1,0:T(8,128)S(1)} %get-tuple-element.37), channel_id=1, source_target_pairs={{0,1},{1,0},{2,3},{3,2},{4,5},{5,4},{6,7},{7,6},{8,9},{9,8},{10,11... | collective-permute-start | bytes 24584 | tf_op jit(solution)/shard_map/ppermute | solution.py:399
  86.0 3.6 %collective-permute-start.10 = (f32[8,256]{1,0:T(8,128)S(1)}, f32[8,256]{1,0:T(8,128)S(1)}, u32[]{:S(2)}, u32[]{:S(2)}) collective-permute-start(f32[8,256]{1,0:T(8,128)S(1)} %add.50.mine), channel_id=1, source_target_pairs={{0,2},{1,3},{2,0},{3,1},{4,6},{5,7},{6,4},{7,5},{8,10},{9,11},{10,... | collective-permute-start | bytes 24584 | tf_op jit(solution)/shard_map/ppermute | solution.py:399
  89.6 6.0 %collective-permute-done.10.other = f32[8,256]{1,0:T(8,128)S(1)} collective-permute-done((f32[8,256]{1,0:T(8,128)S(1)}, f32[8,256]{1,0:T(8,128)S(1)}, u32[]{:S(2)}, u32[]{:S(2)}) %collective-permute-start.10) | collective-permute-done | bytes 8224 | tf_op jit(solution)/shard_map/ppermute | solution.py:399
  96.6 2.1 %collective-permute-start.14 = (bf16[256,1536]{1,0:T(8,128)(2,1)S(1)}, bf16[256,1536]{1,0:T(8,128)(2,1)S(1)}, u32[]{:S(2)}, u32[]{:S(2)}) collective-permute-start(bf16[256,1536]{1,0:T(8,128)(2,1)S(1)} %get-tuple-element.44), channel_id=1, source_target_pairs={{0,4},{4,8},{8,12},{12,16},{16,20},{20,24},{24,28},{28,32},{32,36}... | collective-permute-start | bytes 2359304 | tf_op jit(solution)/shard_map/ppermute | solution.py:411
  98.8 5.5 %backward1.1 = (f32[256,1536]{1,0:T(8,128)S(1)}, f32[3,1536]{1,0:T(4,128)S(1)}, f32[8,256]{1,0:T(8,128)S(1)}) custom-call(bf16[256,1536]{1,0:T(8,128)(2,1)S(1)} %copy-done.3, bf16[256,512]{1,0:T(8,128)(2,1)S(1)} %collective-permute-done.15.dz, bf16[256,1024]{1,0:T(8,128)(2,1)S(1)} %collective-permute-done.16.az, bf16[256,1536]{1,0:T(8,128)(2,1)S(1)} %early_finish0.1.oe, ...), custom_call_target="tpu_custom_call" | custom-call | tf_op jit(solution)/shard_map/backward1/pallas_call | solution.py:214
  105.6 2.3 %collective-permute-start.19 = (f32[8,256]{1,0:T(8,128)S(1)}, f32[8,256]{1,0:T(8,128)S(1)}, u32[]{:S(2)}, u32[]{:S(2)}) collective-permute-start(f32[8,256]{1,0:T(8,128)S(1)} %pad_maximum_fusion.1.late_mine.mine), channel_id=1, source_target_pairs={{0,2},{1,3},{2,0},{3,1},{4,6},{5,7},{6,4},{7,5},{8,10},{9,11},{10,... | collective-permute-start | bytes 24584 | tf_op jit(solution)/shard_map/ppermute | solution.py:397
  108.5 9.0 %collective-permute-done.19.late_other.other = f32[8,256]{1,0:T(8,128)S(1)} collective-permute-done((f32[8,256]{1,0:T(8,128)S(1)}, f32[8,256]{1,0:T(8,128)S(1)}, u32[]{:S(2)}, u32[]{:S(2)}) %collective-permute-start.19) | collective-permute-done | bytes 8224 | tf_op jit(solution)/shard_map/ppermute | solution.py:397
  117.4 2.5 %finish1.1 = bf16[256,1536]{1,0:T(8,128)(2,1)} custom-call(bf16[256,1536]{1,0:T(8,128)(2,1)S(1)} %copy-done.3, bf16[256,512]{1,0:T(8,128)(2,1)S(1)} %collective-permute-done.15.dz, bf16[256,1024]{1,0:T(8,128)(2,1)S(1)} %collective-permute-done.16.az, bf16[256,1536]{1,0:T(8,128)(2,1)S(1)} %early_finish0.1.oe, ...), custom_call_target="tpu_custom_call" | custom-call | tf_op jit(solution)/shard_map/finish1/pallas_call | solution.py:214
  120.2 3.4 %forward1.1 = bf16[256,1536]{1,0:T(8,128)(2,1)} custom-call(bf16[256,1536]{1,0:T(8,128)(2,1)S(1)} %collective-permute-done.14.arrived, bf16[256,1536]{1,0:T(8,128)(2,1)S(1)} %copy-done.1, f32[3,1536]{1,0:T(4,128)S(1)} %bitcast.16, f32[8,256]{1,0:T(8,128)S(1)} %pad_maximum_fusion.1.late_mine.mine, f32[8,256]{1,0:T(8,128)S(1)} %collective-permute-done.19.late_other.other, ...), custom_call_target="tpu_custom_call" | custom-call | tf_op jit(solution)/shard_map/forward1/pallas_call | solution.py:214
  (58 shorter events, 12.7 us)
Async XLA Ops:
  0.6 16.9 %copy-start.6 = (f32[1,3,1536]{2,0,1:T(1,128)S(1)}, f32[1,3,1536]{2,0,1:T(1,128)}, u32[]{:S(2)}) copy-start(f32[1,3,1536]{2,0,1:T(1,128)} %param.14) | copy-start | bytes 55300
  6.6 32.3 %copy-start = (bf16[1,256,1536]{2,1,0:T(8,128)(2,1)S(1)}, bf16[1,256,1536]{2,1,0:T(8,128)(2,1)}, u32[]{:S(2)}) copy-start(bf16[1,256,1536]{2,1,0:T(8,128)(2,1)} %stream.1) | copy-start | bytes 2359300
  6.6 1.5 %collective-permute-start = (f32[16,256]{1,0:T(8,128)}, f32[16,256]{1,0:T(8,128)S(1)}, u32[]{:S(2)}, u32[]{:S(2)}) collective-permute-start(f32[16,256]{1,0:T(8,128)} %get-tuple-element.29), channel_id=1, source_target_pairs={{0,1},{1,0},{2,3},{3,2},{4,5},{5,4},{6,7},{7,6},{8,9},{9,8},{10,11... | collective-permute-start | bytes 49160 | tf_op jit(solution)/shard_map/ppermute | solution.py:397
  8.8 15.2 %collective-permute-start.1 = (f32[16,256]{1,0:T(8,128)S(1)}, f32[16,256]{1,0:T(8,128)S(1)}, u32[]{:S(2)}, u32[]{:S(2)}) collective-permute-start(f32[16,256]{1,0:T(8,128)S(1)} %pad_maximum_fusion.mine.stats_mine), channel_id=1, source_target_pairs={{128,130},{129,131},{130,128},{131,129},{132,134},{133,135},{134,1... | collective-permute-start | bytes 49160 | tf_op jit(solution)/shard_map/ppermute | solution.py:399
  9.5 43.1 %collective-permute-start.5 = (bf16[256,1536]{1,0:T(8,128)(2,1)S(1)}, bf16[256,1536]{1,0:T(8,128)(2,1)S(1)}, u32[]{:S(2)}, u32[]{:S(2)}) collective-permute-start(bf16[256,1536]{1,0:T(8,128)(2,1)S(1)} %bitcast.9), channel_id=1, source_target_pairs={{0,124},{4,0},{8,4},{12,8},{16,12},{20,16},{24,20},{28,24},{32,28}... | collective-permute-start | bytes 2359304 | tf_op jit(solution)/shard_map/ppermute | solution.py:411
  16.3 36.3 %collective-permute-start.4 = (bf16[256,1536]{1,0:T(8,128)(2,1)}, bf16[256,1536]{1,0:T(8,128)(2,1)S(1)}, u32[]{:S(2)}, u32[]{:S(2)}) collective-permute-start(bf16[256,1536]{1,0:T(8,128)(2,1)} %get-tuple-element.33), channel_id=1, source_target_pairs={{252,124},{248,0},{244,4},{240,8},{236,12},{232,16},{228,20},{224,... | collective-permute-start | bytes 2359304 | tf_op jit(solution)/shard_map/ppermute | solution.py:411
  17.6 21.3 %collective-permute-start.3 = (f32[16,256]{1,0:T(8,128)S(1)}, f32[16,256]{1,0:T(8,128)S(1)}, u32[]{:S(2)}, u32[]{:S(2)}) collective-permute-start(f32[16,256]{1,0:T(8,128)S(1)} %pad_maximum_fusion.mine.stats_mine), channel_id=1, source_target_pairs={{0,2},{1,3},{2,0},{3,1},{4,6},{5,7},{6,4},{7,5},{8,10},{9,11},{10,... | collective-permute-start | bytes 49160 | tf_op jit(solution)/shard_map/ppermute | solution.py:399
  25.2 0.7 collective-permute-start.2
  25.9 15.9 %collective-permute-start.8 = (f32[8,256]{1,0:T(8,128)S(1)}, f32[8,256]{1,0:T(8,128)S(1)}, u32[]{:S(2)}, u32[]{:S(2)}) collective-permute-start(f32[8,256]{1,0:T(8,128)S(1)} %add.45.mine), channel_id=1, source_target_pairs={{128,130},{129,131},{130,128},{131,129},{132,134},{133,135},{134,1... | collective-permute-start | bytes 24584 | tf_op jit(solution)/shard_map/ppermute | solution.py:399
  26.6 18.3 %collective-permute-start.6 = (f32[4,256]{1,0:T(4,128)S(1)}, f32[4,256]{1,0:T(4,128)S(1)}, u32[]{:S(2)}, u32[]{:S(2)}) collective-permute-start(f32[4,256]{1,0:T(4,128)S(1)} %pad_maximum_fusion.2), channel_id=1, source_target_pairs={{252,124},{248,0},{244,4},{240,8},{236,12},{232,16},{228,20},{224,... | collective-permute-start | bytes 12296 | tf_op jit(solution)/shard_map/ppermute | solution.py:411
  41.7 39.8 %copy-start.8 = (bf16[256,512]{1,0:T(8,128)(2,1)S(1)}, bf16[256,512]{1,0:T(8,128)(2,1)}, u32[]{:S(2)}) copy-start(bf16[256,512]{1,0:T(8,128)(2,1)} %get-tuple-element.47) | copy-start | bytes 786436
  44.8 23.1 %collective-permute-start.11 = (bf16[256,1024]{1,0:T(8,128)(2,1)S(1)}, bf16[256,1024]{1,0:T(8,128)(2,1)S(1)}, u32[]{:S(2)}, u32[]{:S(2)}) collective-permute-start(bf16[256,1024]{1,0:T(8,128)(2,1)S(1)} %copy-done.7), channel_id=1, source_target_pairs={{252,12},{248,8},{244,4},{240,0},{236,28},{232,24},{228,20},{224,1... | collective-permute-start | bytes 1572872 | tf_op jit(solution)/shard_map/ppermute | solution.py:411
  46.1 52.6 %collective-permute-start.17 = (bf16[256,1536]{1,0:T(8,128)(2,1)S(1)}, bf16[256,1536]{1,0:T(8,128)(2,1)S(1)}, u32[]{:S(2)}, u32[]{:S(2)}) collective-permute-start(bf16[256,1536]{1,0:T(8,128)(2,1)S(1)} %late_finish0.1), channel_id=1, source_target_pairs={{128,124},{132,128},{136,132},{140,136},{144,140},{148,144},{152,1... | collective-permute-start | bytes 2359304 | tf_op jit(solution)/shard_map/ppermute | solution.py:411
  46.8 5.7 %collective-permute-start.7 = (f32[3,1536]{1,0:T(4,128)S(1)}, f32[3,1536]{1,0:T(4,128)S(1)}, u32[]{:S(2)}, u32[]{:S(2)}) collective-permute-start(f32[3,1536]{1,0:T(4,128)S(1)} %bitcast.14), channel_id=1, source_target_pairs={{0,124},{4,0},{8,4},{12,8},{16,12},{20,16},{24,20},{28,24},{32,28}... | collective-permute-start | bytes 55304 | tf_op jit(solution)/shard_map/ppermute | solution.py:411
  57.8 10.2 %collective-permute-start.12 = (f32[4,1536]{1,0:T(4,128)S(1)}, f32[4,1536]{1,0:T(4,128)S(1)}, u32[]{:S(2)}, u32[]{:S(2)}) collective-permute-start(f32[4,1536]{1,0:T(4,128)S(1)} %get-tuple-element.41), channel_id=1, source_target_pairs={{0,4},{4,8},{8,12},{12,16},{16,20},{20,24},{24,28},{28,32},{32,36}... | collective-permute-start | bytes 73736 | tf_op jit(solution)/shard_map/ppermute | solution.py:411
  59.7 8.2 %collective-permute-start.13 = (f32[8,256]{1,0:T(8,128)S(1)}, f32[8,256]{1,0:T(8,128)S(1)}, u32[]{:S(2)}, u32[]{:S(2)}) collective-permute-start(f32[8,256]{1,0:T(8,128)S(1)} %get-tuple-element.42), channel_id=1, source_target_pairs={{0,4},{4,8},{8,12},{12,16},{16,20},{20,24},{24,28},{28,32},{32,36}... | collective-permute-start | bytes 24584 | tf_op jit(solution)/shard_map/ppermute | solution.py:411
  68.0 30.8 %collective-permute-start.16 = (bf16[256,1024]{1,0:T(8,128)(2,1)S(1)}, bf16[256,1024]{1,0:T(8,128)(2,1)S(1)}, u32[]{:S(2)}, u32[]{:S(2)}) collective-permute-start(bf16[256,1024]{1,0:T(8,128)(2,1)S(1)} %collective-permute-done.11), channel_id=1, source_target_pairs={{12,0},{8,4},{4,8},{0,12},{28,16},{24,20},{20,24},{16,28},{44,32},... | collective-permute-start | bytes 1572872 | tf_op jit(solution)/shard_map/ppermute | solution.py:411
  81.6 17.1 %collective-permute-start.15 = (bf16[256,512]{1,0:T(8,128)(2,1)S(1)}, bf16[256,512]{1,0:T(8,128)(2,1)S(1)}, u32[]{:S(2)}, u32[]{:S(2)}) collective-permute-start(bf16[256,512]{1,0:T(8,128)(2,1)S(1)} %copy-done.8), channel_id=1, source_target_pairs={{252,0},{248,4},{244,8},{240,12},{236,16},{232,20},{228,24},{224,2... | collective-permute-start | bytes 786440 | tf_op jit(solution)/shard_map/ppermute | solution.py:411
  82.9 3.1 %collective-permute-start.9 = (f32[8,256]{1,0:T(8,128)S(1)}, f32[8,256]{1,0:T(8,128)S(1)}, u32[]{:S(2)}, u32[]{:S(2)}) collective-permute-start(f32[8,256]{1,0:T(8,128)S(1)} %get-tuple-element.37), channel_id=1, source_target_pairs={{0,1},{1,0},{2,3},{3,2},{4,5},{5,4},{6,7},{7,6},{8,9},{9,8},{10,11... | collective-permute-start | bytes 24584 | tf_op jit(solution)/shard_map/ppermute | solution.py:399
  86.0 12.8 %copy-start.3 = (bf16[256,1536]{1,0:T(8,128)(2,1)S(1)}, bf16[256,1536]{1,0:T(8,128)(2,1)}, u32[]{:S(2)}) copy-start(bf16[256,1536]{1,0:T(8,128)(2,1)} %get-tuple-element.45.oz) | copy-start | bytes 2359300
  86.0 9.7 %collective-permute-start.10 = (f32[8,256]{1,0:T(8,128)S(1)}, f32[8,256]{1,0:T(8,128)S(1)}, u32[]{:S(2)}, u32[]{:S(2)}) collective-permute-start(f32[8,256]{1,0:T(8,128)S(1)} %add.50.mine), channel_id=1, source_target_pairs={{0,2},{1,3},{2,0},{3,1},{4,6},{5,7},{6,4},{7,5},{8,10},{9,11},{10,... | collective-permute-start | bytes 24584 | tf_op jit(solution)/shard_map/ppermute | solution.py:399
  96.6 23.5 %collective-permute-start.14 = (bf16[256,1536]{1,0:T(8,128)(2,1)S(1)}, bf16[256,1536]{1,0:T(8,128)(2,1)S(1)}, u32[]{:S(2)}, u32[]{:S(2)}) collective-permute-start(bf16[256,1536]{1,0:T(8,128)(2,1)S(1)} %get-tuple-element.44), channel_id=1, source_target_pairs={{0,4},{4,8},{8,12},{12,16},{16,20},{20,24},{24,28},{28,32},{32,36}... | collective-permute-start | bytes 2359304 | tf_op jit(solution)/shard_map/ppermute | solution.py:411
  104.3 1.2 %collective-permute-start.18 = (f32[8,256]{1,0:T(8,128)S(1)}, f32[8,256]{1,0:T(8,128)S(1)}, u32[]{:S(2)}, u32[]{:S(2)}) collective-permute-start(f32[8,256]{1,0:T(8,128)S(1)} %add.51), channel_id=1, source_target_pairs={{0,1},{1,0},{2,3},{3,2},{4,5},{5,4},{6,7},{7,6},{8,9},{9,8},{10,11... | collective-permute-start | bytes 24584 | tf_op jit(solution)/shard_map/ppermute | solution.py:397
  105.6 11.9 %collective-permute-start.19 = (f32[8,256]{1,0:T(8,128)S(1)}, f32[8,256]{1,0:T(8,128)S(1)}, u32[]{:S(2)}, u32[]{:S(2)}) collective-permute-start(f32[8,256]{1,0:T(8,128)S(1)} %pad_maximum_fusion.1.late_mine.mine), channel_id=1, source_target_pairs={{0,2},{1,3},{2,0},{3,1},{4,6},{5,7},{6,4},{7,5},{8,10},{9,11},{10,... | collective-permute-start | bytes 24584 | tf_op jit(solution)/shard_map/ppermute | solution.py:397
  (5 other events, 28.6 us)

commit v3 on v2

--- a/solution.py
+++ b/solution.py
@@ -93,29 +93,38 @@
     return jnp.clip(plan[tick, section] - first, 0, 1)
 
 
-def pick_kernel(plan, kept, own, stream, fresh, sent0, direct, around, own0, own1, rows, buffers, sems):
+def pick_kernel(plan, kept, own, stream, fresh, sent0, direct, around, own0, own1, rows, blocks, load_sems, store_sems):
     section, sections = lax.axis_index("pipe"), plan.shape[1]
     cut = direct.shape[1]
     partner = sections - 1 - section
-    copies = [
-        pltpu.make_async_copy(kept.at[0, slot_of(plan, 0, partner, 2)], sent0, sems.at[0]),
-        pltpu.make_async_copy(kept.at[0, slot_of(plan, 1, partner, 2)], buffers.at[0], sems.at[1]),
-        pltpu.make_async_copy(own.at[0, slot_of(plan, 0, section, 0)], own0, sems.at[2]),
-        pltpu.make_async_copy(own.at[0, slot_of(plan, 1, section, 0)], own1, sems.at[3]),
-        pltpu.make_async_copy(stream.at[0], buffers.at[1], sems.at[4]),
-        pltpu.make_async_copy(fresh, buffers.at[2], sems.at[5]),
+    sources = [
+        (KEPT_STASH1, kept.at[0, slot_of(plan, 1, partner, 2)]),
+        (KEPT_STASH0, kept.at[0, slot_of(plan, 0, partner, 2)]),
+        (OWN_STASH0, own.at[0, slot_of(plan, 0, section, 0)]),
+        (OWN_STASH1, own.at[0, slot_of(plan, 1, section, 0)]),
+        (STREAM, stream.at[0]),
+        (FRESH, fresh),
     ]
-    refs = [sent0, buffers.at[0], own0, own1, buffers.at[1], buffers.at[2]]
-    places = (KEPT_STASH0, KEPT_STASH1, OWN_STASH0, OWN_STASH1, STREAM, FRESH)
-    for copy in copies:
-        copy.start()
+    loads = [pltpu.make_async_copy(source, blocks.at[i], load_sems.at[i]) for i, (_, source) in enumerate(sources)]
+    stores = [
+        (0, pltpu.make_async_copy(blocks.at[0, :, pl.ds(0, cut)], direct, store_sems.at[0])),
+        (0, pltpu.make_async_copy(blocks.at[0, :, pl.ds(cut, around.shape[1])], around, store_sems.at[1])),
+        (1, pltpu.make_async_copy(blocks.at[1], sent0, store_sems.at[2])),
+        (2, pltpu.make_async_copy(blocks.at[2], own0, store_sems.at[3])),
+        (3, pltpu.make_async_copy(blocks.at[3], own1, store_sems.at[4])),
+    ]
+    for load in loads:
+        load.start()
     found = {}
-    for place, copy, ref in zip(places, copies, refs):
-        copy.wait()
-        found[place] = moments(ref[...].astype(F32))
+    for i, (place, _) in enumerate(sources):
+        loads[i].wait()
+        for block, store in stores:
+            if block == i:
+                store.start()
+        found[place] = moments(blocks[i].astype(F32))
     rows[...] = statistics_rows(found)
-    direct[...] = buffers[0, :, :cut]
-    around[...] = buffers[0, :, cut:]
+    for _, store in stores:
+        store.wait()
 
 
 def pick(plan, kept, own, stream, fresh):
@@ -125,7 +134,7 @@
     return pl.pallas_call(
         pick_kernel,
         in_specs=[SMEM, HBM, HBM, HBM, HBM],
-        out_specs=[VMEM] * 6,
+        out_specs=[HBM] * 5 + [VMEM],
         out_shape=[
             whole,
             jax.ShapeDtypeStruct((tokens, cut), BF16),
@@ -134,7 +143,11 @@
             whole,
             jax.ShapeDtypeStruct((16, tokens), F32),
         ],
-        scratch_shapes=[pltpu.VMEM((3, tokens, width), BF16), pltpu.SemaphoreType.DMA((6,))],
+        scratch_shapes=[
+            pltpu.VMEM((6, tokens, width), BF16),
+            pltpu.SemaphoreType.DMA((6,)),
+            pltpu.SemaphoreType.DMA((5,)),
+        ],
         compiler_params=ALL_VMEM,
         name="pick",
     )(plan, kept, own, stream, fresh)
@@ -200,14 +213,20 @@
     rows[...] = to_rows([None, None, total, squares])
 
 
-def forward1_kernel(arrived, fresh, gains, late_mine, late_other, mine, other, out, mean, rstd):
-    first = lax.axis_index("pipe") == 0
+def forward1_kernel(low, high, fresh, gains, late_mine, late_other, mine, other, out, mean, rstd):
+    section = lax.axis_index("pipe")
+    first = section == 0
+    from_low = section <= lax.axis_size("pipe") // 2
     width = out.shape[1]
     norm = [
         jnp.where(first, a, b)
         for a, b in zip(statistics_norm(mine, other, FRESH, width), gradients_norm(late_mine, late_other, width))
     ]
-    forward_body(lambda at: jnp.where(first, fresh[:, at], arrived[:, at]), gains, norm, out, mean, rstd)
+
+    def pick(at):
+        return jnp.where(first, fresh[:, at], jnp.where(from_low, low[:, at], high[:, at]))
+
+    forward_body(pick, gains, norm, out, mean, rstd)
 
 
 def local_call(kernel, out_shape, scratch, operands, name):
@@ -399,6 +418,14 @@
     return lax.ppermute(value, ("pipe", "tp"), pairs)
 
 
+def kept_statistics(both):
+    return jnp.concatenate([both[KEPT_STASH0 : KEPT_STASH1 + 1], both[KEPT_STASH0 + 8 : KEPT_STASH1 + 9]])
+
+
+def with_other_core(value, sections=None):
+    return value + over_tp(value, 1, sections)
+
+
 def per_device(
     stream_in, grad_in, fresh_batch, loss_grad, local_stash, partner_stash, norm_gains, stash_plan
 ):
@@ -415,57 +442,57 @@
 
     half = lax.axis_size("pipe") // 2
     low, high = range(half), range(half, 2 * half)
-    sent0, direct, around, own_z0, own_z1, rows = pick(
-        stash_plan, partner_stash, local_stash, stream_in, fresh_batch
-    )
-    got_z0 = moved(sent0, stash_ahead)
+    sent0, direct, around, own_z0, own_z1, rows0 = pick(stash_plan, partner_stash, local_stash, stream_in, fresh_batch)
+    stats_mine = join_statistics(rows0, over_tp(rows0, 1), width)
+    late_other = over_tp(stats_mine, 2, high)
+    low_other = over_tp(stats_mine, 2, low)
+    late_stats = (stats_mine, late_other)
+    stats = (stats_mine, late_other + low_other)
+    kept_rows = kept_statistics(join_statistics(*late_stats, half_count(width)))
+    got_gains = moved(gains, early_back)
     got_e0 = moved(cotangent, early_back)
-    got_gains = moved(gains, early_back)
-    stats_mine = join_statistics(rows, over_tp(rows, 1), width)
-    late_other = over_tp(stats_mine, 2, high)
-    late_stats = (stats_mine, late_other)
-    both = join_statistics(*late_stats, half_count(width))
-    kept = [both[place : place + 1] for place in (KEPT_STASH0, KEPT_STASH1, KEPT_STASH0 + 8, KEPT_STASH1 + 8)]
-    got_stats = moved(jnp.concatenate(kept), stash_ahead)
-    stats = (stats_mine, late_other + over_tp(stats_mine, 2, low))
-
-    late_tick0 = (own_z0, cotangent)
-    grad, late_part, sums = backward(late_backward0_kernel, "late_backward0", 3, *late_tick0, gains, *late_stats)
-    sums_mine = sums + over_tp(sums, 1, high)
-    sums_other = over_tp(sums_mine, 2, high)
-    produced, out_rows = forward(forward0_kernel, "forward0", True, after(stream_in[0], sums_mine), gains, *stats)
-    grad = after(grad, produced)
+    got_z0 = moved(after(sent0, stats_mine), stash_ahead)
+    got_stats = moved(kept_rows, stash_ahead)
+    crossed = moved(around, across)
+    got_z1b = moved(crossed, along)
+    late_grad, late_part, late_sums = backward(
+        late_backward0_kernel, "late_backward0", 3, own_z0, cotangent, after(gains, got_gains, crossed), *late_stats
+    )
+    late_mine = with_other_core(late_sums)
+    got_z1a = moved(after(direct, late_mine), mirrored)
+    late_sums_other = over_tp(late_mine, 2, high)
+    produced, out_rows = forward(
+        forward0_kernel, "forward0", True, after(stream_in[0], late_mine), gains, *stats
+    )
+    got_out_rows = moved(out_rows, to_next)
     late_returned = finish(
-        late_finish0_kernel, "late_finish0", *late_tick0, *late_stats, sums_mine, sums_other, grad
+        late_finish0_kernel, "late_finish0", own_z0, cotangent, *late_stats, late_mine, late_sums_other,
+        after(late_grad, got_stats, produced)
     )
     came_back = moved(late_returned, late_back)
-    got_out_rows = moved(out_rows, to_next)
-    around = moved(after(around, got_stats, late_returned), across)
-    got_z1a = moved(after(direct, got_stats, late_returned), mirrored)
-
-    early_tick0 = (got_z0, got_e0)
-    grad, early_part, sums = backward(
-        early_backward0_kernel, "early_backward0", 4, *early_tick0, got_gains, after(got_stats, late_returned)
+    early_grad, early_part, early_sums = backward(
+        early_backward0_kernel, "early_backward0", 4, got_z0, got_e0, got_gains,
+        after(got_stats, late_returned)
     )
     gain_back = moved(early_part, early_on)
-    sums_mine = sums + over_tp(sums, 1, low)
-    sums_other = over_tp(sums_mine, 2, low)
-    grad, around = lax.optimization_barrier((grad, around, gain_back, got_out_rows))[:2]
+    early_mine = with_other_core(early_sums)
+    early_sums_other = over_tp(early_mine, 2, low)
     early_returned = finish(
-        early_finish0_kernel, "early_finish0", *early_tick0, got_stats, sums_mine, sums_other, grad
-    )
-    got_z1b = moved(around, along)
-    arrived = moved(after(produced, early_returned), to_next)
-
+        early_finish0_kernel, "early_finish0", got_z0, got_e0, got_stats, early_mine, early_sums_other,
+        after(early_grad, gain_back)
+    )
+    arrived = moved(after(produced, early_returned, got_out_rows), to_next)
     tick1 = (own_z1, got_z1a, got_z1b, early_returned, came_back, loss_grad)
-    grad, gain_total, sums = backward(
+    last_grad, gain_total, last_sums = backward(
         backward1_kernel, "backward1", 3, *tick1, gains, late_part, gain_back, *late_stats
     )
-    rows = sums + got_out_rows
-    sums_mine = join_gradients(rows, over_tp(rows, 1), width)
-    sums1 = (sums_mine, over_tp(sums_mine, 2))
-    fwd_out = forward(forward1_kernel, "forward1", False, arrived, fresh_batch, gains, *sums1, *stats)[0]
-    bwd_out = finish(finish1_kernel, "finish1", *tick1, *late_stats, gain_back, *sums1, grad)
+    rows1 = last_sums + got_out_rows
+    rows1_mine = join_gradients(rows1, over_tp(rows1, 1), width)
+    sums1 = (rows1_mine, over_tp(rows1_mine, 2))
+    fwd_out = forward(
+        forward1_kernel, "forward1", False, arrived, arrived, fresh_batch, gains, *sums1, *stats
+    )[0]
+    bwd_out = finish(finish1_kernel, "finish1", *tick1, *late_stats, gain_back, *sums1, last_grad)
     return (fwd_out[None], bwd_out[None], gain_total[None])
 
 

time: 124 us -> 119 us (0.960)
  the two profiles are of different devices: /device:TPU:6 before, /device:TPU:36 now
where the time goes in v3:
time: 119 us; the launch traced here: 118 us
  waiting for transfers between devices  46.6 us (39%)
  starting transfers between devices  41.7 us (35%)
  Pallas kernels  26.3 us (22%)
  local copies, waits for them, and re-layouts  1.8 us (2%)
    ppermute x11, starting transfers between devices, moved(): return lax.ppermute(value, 'pipe', pairs)  30.6 us
    ppermute x11, waiting for transfers between devices, moved(): return lax.ppermute(value, 'pipe', pairs)  25.6 us
    pallas_call x8, Pallas kernels, local_call(): pl.pallas_call(kernel, in_specs=[VMEM] * len(operands), out_specs=[VMEM]...  20.7 us
    ppermute x4, starting transfers between devices, over_tp(): return lax.ppermute(value, ('pipe', 'tp'), pairs)  10.8 us
    ppermute x4, waiting for transfers between devices, over_tp(): return lax.ppermute(value, ('pipe', 'tp'), pairs)  10.6 us
    ppermute x5, waiting for transfers between devices, over_tp(): return lax.ppermute(value, 'tp', [(i, i ^ mask) for i in range(PARTS)])  10.4 us
    pallas_call x1, Pallas kernels, pick(): pl.pallas_call(pick_kernel, in_specs=[SMEM, HBM, HBM, HBM, HBM], out_spec...  5.62 us
  transfers between devices with their start and end apart: 20, of which 9 were waited for; matrix products, arithmetic and copies ran while one was open for 1% of the time, Pallas kernels for 15%

profile of v3, /device:TPU:36, one launch (start us, length us, event | category | flops | bytes accessed | tf_op | source)
XLA Modules:
  0.0 118.2 jit_solution(3285895041146660287)
XLA Ops:
  0.7 5.6 %pick.1 = (bf16[256,1536]{1,0:T(8,128)(2,1)}, bf16[256,512]{1,0:T(8,128)(2,1)}, bf16[256,1024]{1,0:T(8,128)(2,1)}, bf16[256,1536]{1,0:T(8,128)(2,1)}, bf16[256,1536]{1,0:T(8,128)(2,1)}, /*index=5*/f32[16,256]{1,0:T(8,128)}) custom-call(s32[2,64]{1,0:T(2,128)} %plan.1, bf16[1,2,256,1536]{3,2,1,0:T(8,128)(2,1)} %kept.1, bf16[1,2,256,1536]{3,2,1,0:T(8,128)(2,1)} %own.1, ...), custom_call_target="tpu_custom_call" | custom-call | tf_op jit(solution)/shard_map/pick/pallas_call | solution.py:134
  6.4 1.4 %collective-permute-start.1 = (bf16[256,1024]{1,0:T(8,128)(2,1)}, bf16[256,1024]{1,0:T(8,128)(2,1)S(1)}, u32[]{:S(2)}, u32[]{:S(2)}) collective-permute-start(bf16[256,1024]{1,0:T(8,128)(2,1)} %get-tuple-element.29), channel_id=1, source_target_pairs={{252,12},{248,8},{244,4},{240,0},{236,28},{232,24},{228,20},{224,1... | collective-permute-start | bytes 1572872 | tf_op jit(solution)/shard_map/ppermute | solution.py:438
  9.3 2.0 %collective-permute-start = (f32[3,1536]{1,0:T(4,128)S(1)}, f32[3,1536]{1,0:T(4,128)S(1)}, u32[]{:S(2)}, u32[]{:S(2)}) collective-permute-start(f32[3,1536]{1,0:T(4,128)S(1)} %bitcast.12), channel_id=1, source_target_pairs={{0,124},{4,0},{8,4},{12,8},{16,12},{20,16},{24,20},{28,24},{32,28}... | collective-permute-start | bytes 55304 | tf_op jit(solution)/shard_map/ppermute | solution.py:438
  11.3 6.5 %collective-permute-start.7 = (bf16[256,1536]{1,0:T(8,128)(2,1)S(1)}, bf16[256,1536]{1,0:T(8,128)(2,1)S(1)}, u32[]{:S(2)}, u32[]{:S(2)}) collective-permute-start(bf16[256,1536]{1,0:T(8,128)(2,1)S(1)} %bitcast.9), channel_id=1, source_target_pairs={{0,124},{4,0},{8,4},{12,8},{16,12},{20,16},{24,20},{28,24},{32,28}... | collective-permute-start | bytes 2359304 | tf_op jit(solution)/shard_map/ppermute | solution.py:438
  17.8 6.4 %collective-permute-start.5 = (f32[16,256]{1,0:T(8,128)S(1)}, f32[16,256]{1,0:T(8,128)S(1)}, u32[]{:S(2)}, u32[]{:S(2)}) collective-permute-start(f32[16,256]{1,0:T(8,128)S(1)} %pad_maximum_fusion.mine.stats_mine), channel_id=1, source_target_pairs={{0,2},{1,3},{2,0},{3,1},{4,6},{5,7},{6,4},{7,5},{8,10},{9,11},{10,... | collective-permute-start | bytes 49160 | tf_op jit(solution)/shard_map/ppermute | solution.py:418
  24.2 1.3 %collective-permute-start.6 = (bf16[256,1536]{1,0:T(8,128)(2,1)}, bf16[256,1536]{1,0:T(8,128)(2,1)S(1)}, u32[]{:S(2)}, u32[]{:S(2)}) collective-permute-start(bf16[256,1536]{1,0:T(8,128)(2,1)} %get-tuple-element.36), channel_id=1, source_target_pairs={{252,124},{248,0},{244,4},{240,8},{236,12},{232,16},{228,20},{224,... | collective-permute-start | bytes 2359304 | tf_op jit(solution)/shard_map/ppermute | solution.py:438
  28.5 1.3 %collective-permute-start.8 = (f32[4,256]{1,0:T(4,128)S(1)}, f32[4,256]{1,0:T(4,128)S(1)}, u32[]{:S(2)}, u32[]{:S(2)}) collective-permute-start(f32[4,256]{1,0:T(4,128)S(1)} %pad_maximum_fusion.2), channel_id=1, source_target_pairs={{252,124},{248,0},{244,4},{240,8},{236,12},{232,16},{228,20},{224,... | collective-permute-start | bytes 12296 | tf_op jit(solution)/shard_map/ppermute | solution.py:438
  29.8 10.6 %collective-permute-done.5 = f32[16,256]{1,0:T(8,128)S(1)} collective-permute-done((f32[16,256]{1,0:T(8,128)S(1)}, f32[16,256]{1,0:T(8,128)S(1)}, u32[]{:S(2)}, u32[]{:S(2)}) %collective-permute-start.5) | collective-permute-done | bytes 16416 | tf_op jit(solution)/shard_map/ppermute | solution.py:418
  40.5 2.8 %forward0.1 = (bf16[256,1536]{1,0:T(8,128)(2,1)S(1)}, f32[8,256]{1,0:T(8,128)S(1)}) custom-call(bf16[256,1536]{1,0:T(8,128)(2,1)S(1)} %bitcast.8, f32[3,1536]{1,0:T(4,128)S(1)} %bitcast.14, f32[16,256]{1,0:T(8,128)S(1)} %pad_maximum_fusion.mine.stats_mine, f32[16,256]{1,0:T(8,128)S(1)} %add.46.other), custom_call_target="tpu_custom_call" | custom-call | tf_op jit(solution)/shard_map/forward0/pallas_call | solution.py:233
  43.3 4.2 %collective-permute-done.8.got_stats = f32[4,256]{1,0:T(4,128)S(1)} collective-permute-done((f32[4,256]{1,0:T(4,128)S(1)}, f32[4,256]{1,0:T(4,128)S(1)}, u32[]{:S(2)}, u32[]{:S(2)}) %collective-permute-start.8) | collective-permute-done | bytes 4128 | tf_op jit(solution)/shard_map/ppermute | solution.py:438
  48.3 4.2 %collective-permute-start.16 = (bf16[256,1024]{1,0:T(8,128)(2,1)S(1)}, bf16[256,1024]{1,0:T(8,128)(2,1)S(1)}, u32[]{:S(2)}, u32[]{:S(2)}) collective-permute-start(bf16[256,1024]{1,0:T(8,128)(2,1)S(1)} %collective-permute-done.1), channel_id=1, source_target_pairs={{12,0},{8,4},{4,8},{0,12},{28,16},{24,20},{20,24},{16,28},{44,32},... | collective-permute-start | bytes 1572872 | tf_op jit(solution)/shard_map/ppermute | solution.py:438
  52.5 1.3 %collective-permute-start.15 = (bf16[256,512]{1,0:T(8,128)(2,1)S(1)}, bf16[256,512]{1,0:T(8,128)(2,1)S(1)}, u32[]{:S(2)}, u32[]{:S(2)}) collective-permute-start(bf16[256,512]{1,0:T(8,128)(2,1)S(1)} %copy-done.7), channel_id=1, source_target_pairs={{252,0},{248,4},{244,8},{240,12},{236,16},{232,20},{228,24},{224,2... | collective-permute-start | bytes 786440 | tf_op jit(solution)/shard_map/ppermute | solution.py:438
  53.9 5.3 %early_backward0.1 = (f32[256,1536]{1,0:T(8,128)S(1)}, f32[4,1536]{1,0:T(4,128)S(1)}, f32[8,256]{1,0:T(8,128)S(1)}) custom-call(bf16[256,1536]{1,0:T(8,128)(2,1)S(1)} %collective-permute-done.6.z, bf16[256,1536]{1,0:T(8,128)(2,1)S(1)} %collective-permute-done.7.e, f32[3,1536]{1,0:T(4,128)S(1)} %collective-permute-done.gains, ...), custom_call_target="tpu_custom_call" | custom-call | tf_op jit(solution)/shard_map/early_backward0/pallas_call | solution.py:233
  59.1 1.9 %collective-permute-start.12 = (f32[4,1536]{1,0:T(4,128)S(1)}, f32[4,1536]{1,0:T(4,128)S(1)}, u32[]{:S(2)}, u32[]{:S(2)}) collective-permute-start(f32[4,1536]{1,0:T(4,128)S(1)} %get-tuple-element.42), channel_id=1, source_target_pairs={{0,4},{4,8},{8,12},{12,16},{16,20},{20,24},{24,28},{28,32},{32,36}... | collective-permute-start | bytes 73736 | tf_op jit(solution)/shard_map/ppermute | solution.py:438
  61.1 1.2 collective-permute-done.10
  62.3 3.1 %collective-permute-start.11 = (f32[8,256]{1,0:T(8,128)S(1)}, f32[8,256]{1,0:T(8,128)S(1)}, u32[]{:S(2)}, u32[]{:S(2)}) collective-permute-start(f32[8,256]{1,0:T(8,128)S(1)} %add.50.mine), channel_id=1, source_target_pairs={{0,2},{1,3},{2,0},{3,1},{4,6},{5,7},{6,4},{7,5},{8,10},{9,11},{10,... | collective-permute-start | bytes 24584 | tf_op jit(solution)/shard_map/ppermute | solution.py:418
  65.4 9.1 %collective-permute-done.12.got_part = f32[4,1536]{1,0:T(4,128)S(1)} collective-permute-done((f32[4,1536]{1,0:T(4,128)S(1)}, f32[4,1536]{1,0:T(4,128)S(1)}, u32[]{:S(2)}, u32[]{:S(2)}) %collective-permute-start.12) | collective-permute-done | bytes 24608 | tf_op jit(solution)/shard_map/ppermute | solution.py:438
  74.5 4.4 %collective-permute-start.13 = (f32[8,256]{1,0:T(8,128)S(1)}, f32[8,256]{1,0:T(8,128)S(1)}, u32[]{:S(2)}, u32[]{:S(2)}) collective-permute-start(f32[8,256]{1,0:T(8,128)S(1)} %get-tuple-element.44), channel_id=1, source_target_pairs={{0,4},{4,8},{8,12},{12,16},{16,20},{20,24},{24,28},{28,32},{32,36}... | collective-permute-start | bytes 24584 | tf_op jit(solution)/shard_map/ppermute | solution.py:438
  80.2 5.5 %collective-permute-start.14 = (bf16[256,1536]{1,0:T(8,128)(2,1)S(1)}, bf16[256,1536]{1,0:T(8,128)(2,1)S(1)}, u32[]{:S(2)}, u32[]{:S(2)}) collective-permute-start(bf16[256,1536]{1,0:T(8,128)(2,1)S(1)} %get-tuple-element.45), channel_id=1, source_target_pairs={{0,4},{4,8},{8,12},{12,16},{16,20},{20,24},{24,28},{28,32},{32,36}... | collective-permute-start | bytes 2359304 | tf_op jit(solution)/shard_map/ppermute | solution.py:438
  85.7 12.1 %collective-permute-done.15.dz = bf16[256,512]{1,0:T(8,128)(2,1)S(1)} collective-permute-done((bf16[256,512]{1,0:T(8,128)(2,1)S(1)}, bf16[256,512]{1,0:T(8,128)(2,1)S(1)}, u32[]{:S(2)}, u32[]{:S(2)}) %collective-permute-start.15) | collective-permute-done | bytes 262176 | tf_op jit(solution)/shard_map/ppermute | solution.py:438
  97.8 5.5 %backward1.1 = (f32[256,1536]{1,0:T(8,128)S(1)}, f32[3,1536]{1,0:T(4,128)S(1)}, f32[8,256]{1,0:T(8,128)S(1)}) custom-call(bf16[256,1536]{1,0:T(8,128)(2,1)S(1)} %copy-done.3, bf16[256,512]{1,0:T(8,128)(2,1)S(1)} %collective-permute-done.15.dz, bf16[256,1024]{1,0:T(8,128)(2,1)S(1)} %collective-permute-done.16.az, bf16[256,1536]{1,0:T(8,128)(2,1)S(1)} %early_finish0.1.oe, ...), custom_call_target="tpu_custom_call" | custom-call | tf_op jit(solution)/shard_map/backward1/pallas_call | solution.py:233
  105.3 7.0 %collective-permute-done.19.late_other.other = f32[8,256]{1,0:T(8,128)S(1)} collective-permute-done((f32[8,256]{1,0:T(8,128)S(1)}, f32[8,256]{1,0:T(8,128)S(1)}, u32[]{:S(2)}, u32[]{:S(2)}) %collective-permute-start.19) | collective-permute-done | bytes 8224 | tf_op jit(solution)/shard_map/ppermute | solution.py:416
  112.3 2.5 %finish1.1 = bf16[256,1536]{1,0:T(8,128)(2,1)} custom-call(bf16[256,1536]{1,0:T(8,128)(2,1)S(1)} %copy-done.3, bf16[256,512]{1,0:T(8,128)(2,1)S(1)} %collective-permute-done.15.dz, bf16[256,1024]{1,0:T(8,128)(2,1)S(1)} %collective-permute-done.16.az, bf16[256,1536]{1,0:T(8,128)(2,1)S(1)} %early_finish0.1.oe, ...), custom_call_target="tpu_custom_call" | custom-call | tf_op jit(solution)/shard_map/finish1/pallas_call | solution.py:233
  114.8 3.5 %forward1.1 = bf16[256,1536]{1,0:T(8,128)(2,1)} custom-call(bf16[256,1536]{1,0:T(8,128)(2,1)S(1)} %collective-permute-done.14.low.high, bf16[256,1536]{1,0:T(8,128)(2,1)S(1)} %collective-permute-done.14.low.high, bf16[256,1536]{1,0:T(8,128)(2,1)S(1)} %copy-done.1, f32[3,1536]{1,0:T(4,128)S(1)} %bitcast.16, f32[8,256]{1,0:T(8,128)S(1)} %pad_maximum_fusion.1.late_mine.mine, ...), custom_call_target="tpu_custom_call" | custom-call | tf_op jit(solution)/shard_map/forward1/pallas_call | solution.py:233
  (56 shorter events, 8.7 us)
Async XLA Ops:
  0.6 10.6 %copy-start.4 = (bf16[1,256,1536]{2,1,0:T(8,128)(2,1)S(1)}, bf16[1,256,1536]{2,1,0:T(8,128)(2,1)}, u32[]{:S(2)}) copy-start(bf16[1,256,1536]{2,1,0:T(8,128)(2,1)} %param.9) | copy-start | bytes 2359300
  6.3 34.2 %copy-start = (bf16[1,256,1536]{2,1,0:T(8,128)(2,1)S(1)}, bf16[1,256,1536]{2,1,0:T(8,128)(2,1)}, u32[]{:S(2)}) copy-start(bf16[1,256,1536]{2,1,0:T(8,128)(2,1)} %stream.1) | copy-start | bytes 2359300
  6.3 1.5 %collective-permute-start.2 = (f32[16,256]{1,0:T(8,128)}, f32[16,256]{1,0:T(8,128)S(1)}, u32[]{:S(2)}, u32[]{:S(2)}) collective-permute-start(f32[16,256]{1,0:T(8,128)} %get-tuple-element.31), channel_id=1, source_target_pairs={{0,1},{1,0},{2,3},{3,2},{4,5},{5,4},{6,7},{7,6},{8,9},{9,8},{10,11... | collective-permute-start | bytes 49160 | tf_op jit(solution)/shard_map/ppermute | solution.py:416
  6.4 19.2 %collective-permute-start.1 = (bf16[256,1024]{1,0:T(8,128)(2,1)}, bf16[256,1024]{1,0:T(8,128)(2,1)S(1)}, u32[]{:S(2)}, u32[]{:S(2)}) collective-permute-start(bf16[256,1024]{1,0:T(8,128)(2,1)} %get-tuple-element.29), channel_id=1, source_target_pairs={{252,12},{248,8},{244,4},{240,0},{236,28},{232,24},{228,20},{224,1... | collective-permute-start | bytes 1572872 | tf_op jit(solution)/shard_map/ppermute | solution.py:438
  8.6 15.7 %collective-permute-start.3 = (f32[16,256]{1,0:T(8,128)S(1)}, f32[16,256]{1,0:T(8,128)S(1)}, u32[]{:S(2)}, u32[]{:S(2)}) collective-permute-start(f32[16,256]{1,0:T(8,128)S(1)} %pad_maximum_fusion.mine.stats_mine), channel_id=1, source_target_pairs={{128,130},{129,131},{130,128},{131,129},{132,134},{133,135},{134,1... | collective-permute-start | bytes 49160 | tf_op jit(solution)/shard_map/ppermute | solution.py:418
  9.3 16.3 %collective-permute-start = (f32[3,1536]{1,0:T(4,128)S(1)}, f32[3,1536]{1,0:T(4,128)S(1)}, u32[]{:S(2)}, u32[]{:S(2)}) collective-permute-start(f32[3,1536]{1,0:T(4,128)S(1)} %bitcast.12), channel_id=1, source_target_pairs={{0,124},{4,0},{8,4},{12,8},{16,12},{20,16},{24,20},{28,24},{32,28}... | collective-permute-start | bytes 55304 | tf_op jit(solution)/shard_map/ppermute | solution.py:438
  11.3 42.5 %collective-permute-start.7 = (bf16[256,1536]{1,0:T(8,128)(2,1)S(1)}, bf16[256,1536]{1,0:T(8,128)(2,1)S(1)}, u32[]{:S(2)}, u32[]{:S(2)}) collective-permute-start(bf16[256,1536]{1,0:T(8,128)(2,1)S(1)} %bitcast.9), channel_id=1, source_target_pairs={{0,124},{4,0},{8,4},{12,8},{16,12},{20,16},{24,20},{28,24},{32,28}... | collective-permute-start | bytes 2359304 | tf_op jit(solution)/shard_map/ppermute | solution.py:438
  17.8 22.7 %collective-permute-start.5 = (f32[16,256]{1,0:T(8,128)S(1)}, f32[16,256]{1,0:T(8,128)S(1)}, u32[]{:S(2)}, u32[]{:S(2)}) collective-permute-start(f32[16,256]{1,0:T(8,128)S(1)} %pad_maximum_fusion.mine.stats_mine), channel_id=1, source_target_pairs={{0,2},{1,3},{2,0},{3,1},{4,6},{5,7},{6,4},{7,5},{8,10},{9,11},{10,... | collective-permute-start | bytes 49160 | tf_op jit(solution)/shard_map/ppermute | solution.py:418
  24.2 29.6 %collective-permute-start.6 = (bf16[256,1536]{1,0:T(8,128)(2,1)}, bf16[256,1536]{1,0:T(8,128)(2,1)S(1)}, u32[]{:S(2)}, u32[]{:S(2)}) collective-permute-start(bf16[256,1536]{1,0:T(8,128)(2,1)} %get-tuple-element.36), channel_id=1, source_target_pairs={{252,124},{248,0},{244,4},{240,8},{236,12},{232,16},{228,20},{224,... | collective-permute-start | bytes 2359304 | tf_op jit(solution)/shard_map/ppermute | solution.py:438
  26.7 1.2 collective-permute-start.4
  27.9 19.6 %collective-permute-start.9 = (f32[8,256]{1,0:T(8,128)S(1)}, f32[8,256]{1,0:T(8,128)S(1)}, u32[]{:S(2)}, u32[]{:S(2)}) collective-permute-start(f32[8,256]{1,0:T(8,128)S(1)} %add.45.mine), channel_id=1, source_target_pairs={{128,130},{129,131},{130,128},{131,129},{132,134},{133,135},{134,1... | collective-permute-start | bytes 24584 | tf_op jit(solution)/shard_map/ppermute | solution.py:418
  28.5 18.9 %collective-permute-start.8 = (f32[4,256]{1,0:T(4,128)S(1)}, f32[4,256]{1,0:T(4,128)S(1)}, u32[]{:S(2)}, u32[]{:S(2)}) collective-permute-start(f32[4,256]{1,0:T(4,128)S(1)} %pad_maximum_fusion.2), channel_id=1, source_target_pairs={{252,124},{248,0},{244,4},{240,8},{236,12},{232,16},{228,20},{224,... | collective-permute-start | bytes 12296 | tf_op jit(solution)/shard_map/ppermute | solution.py:438
  47.5 50.3 %collective-permute-start.17 = (bf16[256,1536]{1,0:T(8,128)(2,1)S(1)}, bf16[256,1536]{1,0:T(8,128)(2,1)S(1)}, u32[]{:S(2)}, u32[]{:S(2)}) collective-permute-start(bf16[256,1536]{1,0:T(8,128)(2,1)S(1)} %late_finish0.1), channel_id=1, source_target_pairs={{128,124},{132,128},{136,132},{140,136},{144,140},{148,144},{152,1... | collective-permute-start | bytes 2359304 | tf_op jit(solution)/shard_map/ppermute | solution.py:438
  48.3 49.5 %collective-permute-start.16 = (bf16[256,1024]{1,0:T(8,128)(2,1)S(1)}, bf16[256,1024]{1,0:T(8,128)(2,1)S(1)}, u32[]{:S(2)}, u32[]{:S(2)}) collective-permute-start(bf16[256,1024]{1,0:T(8,128)(2,1)S(1)} %collective-permute-done.1), channel_id=1, source_target_pairs={{12,0},{8,4},{4,8},{0,12},{28,16},{24,20},{20,24},{16,28},{44,32},... | collective-permute-start | bytes 1572872 | tf_op jit(solution)/shard_map/ppermute | solution.py:438
  52.5 45.3 %collective-permute-start.15 = (bf16[256,512]{1,0:T(8,128)(2,1)S(1)}, bf16[256,512]{1,0:T(8,128)(2,1)S(1)}, u32[]{:S(2)}, u32[]{:S(2)}) collective-permute-start(bf16[256,512]{1,0:T(8,128)(2,1)S(1)} %copy-done.7), channel_id=1, source_target_pairs={{252,0},{248,4},{244,8},{240,12},{236,16},{232,20},{228,24},{224,2... | collective-permute-start | bytes 786440 | tf_op jit(solution)/shard_map/ppermute | solution.py:438
  59.1 15.4 %collective-permute-start.12 = (f32[4,1536]{1,0:T(4,128)S(1)}, f32[4,1536]{1,0:T(4,128)S(1)}, u32[]{:S(2)}, u32[]{:S(2)}) collective-permute-start(f32[4,1536]{1,0:T(4,128)S(1)} %get-tuple-element.42), channel_id=1, source_target_pairs={{0,4},{4,8},{8,12},{12,16},{16,20},{20,24},{24,28},{28,32},{32,36}... | collective-permute-start | bytes 73736 | tf_op jit(solution)/shard_map/ppermute | solution.py:438
  61.0 1.3 %collective-permute-start.10 = (f32[8,256]{1,0:T(8,128)S(1)}, f32[8,256]{1,0:T(8,128)S(1)}, u32[]{:S(2)}, u32[]{:S(2)}) collective-permute-start(f32[8,256]{1,0:T(8,128)S(1)} %get-tuple-element.40), channel_id=1, source_target_pairs={{0,1},{1,0},{2,3},{3,2},{4,5},{5,4},{6,7},{7,6},{8,9},{9,8},{10,11... | collective-permute-start | bytes 24584 | tf_op jit(solution)/shard_map/ppermute | solution.py:416
  62.3 16.6 %collective-permute-start.11 = (f32[8,256]{1,0:T(8,128)S(1)}, f32[8,256]{1,0:T(8,128)S(1)}, u32[]{:S(2)}, u32[]{:S(2)}) collective-permute-start(f32[8,256]{1,0:T(8,128)S(1)} %add.50.mine), channel_id=1, source_target_pairs={{0,2},{1,3},{2,0},{3,1},{4,6},{5,7},{6,4},{7,5},{8,10},{9,11},{10,... | collective-permute-start | bytes 24584 | tf_op jit(solution)/shard_map/ppermute | solution.py:418
  74.5 5.7 %collective-permute-start.13 = (f32[8,256]{1,0:T(8,128)S(1)}, f32[8,256]{1,0:T(8,128)S(1)}, u32[]{:S(2)}, u32[]{:S(2)}) collective-permute-start(f32[8,256]{1,0:T(8,128)S(1)} %get-tuple-element.44), channel_id=1, source_target_pairs={{0,4},{4,8},{8,12},{12,16},{16,20},{20,24},{24,28},{28,32},{32,36}... | collective-permute-start | bytes 24584 | tf_op jit(solution)/shard_map/ppermute | solution.py:438
  78.9 18.9 %copy-start.2 = (bf16[256,1536]{1,0:T(8,128)(2,1)S(1)}, bf16[256,1536]{1,0:T(8,128)(2,1)}, u32[]{:S(2)}) copy-start(bf16[256,1536]{1,0:T(8,128)(2,1)} %le.3) | copy-start | bytes 2359300
  78.9 18.9 %copy-start.3 = (bf16[256,1536]{1,0:T(8,128)(2,1)S(1)}, bf16[256,1536]{1,0:T(8,128)(2,1)}, u32[]{:S(2)}) copy-start(bf16[256,1536]{1,0:T(8,128)(2,1)} %get-tuple-element.46.oz) | copy-start | bytes 2359300
  80.2 34.6 %collective-permute-start.14 = (bf16[256,1536]{1,0:T(8,128)(2,1)S(1)}, bf16[256,1536]{1,0:T(8,128)(2,1)S(1)}, u32[]{:S(2)}, u32[]{:S(2)}) collective-permute-start(bf16[256,1536]{1,0:T(8,128)(2,1)S(1)} %get-tuple-element.45), channel_id=1, source_target_pairs={{0,4},{4,8},{8,12},{12,16},{16,20},{20,24},{24,28},{28,32},{32,36}... | collective-permute-start | bytes 2359304 | tf_op jit(solution)/shard_map/ppermute | solution.py:438
  103.3 1.2 %collective-permute-start.18 = (f32[8,256]{1,0:T(8,128)S(1)}, f32[8,256]{1,0:T(8,128)S(1)}, u32[]{:S(2)}, u32[]{:S(2)}) collective-permute-start(f32[8,256]{1,0:T(8,128)S(1)} %add.51), channel_id=1, source_target_pairs={{0,1},{1,0},{2,3},{3,2},{4,5},{5,4},{6,7},{7,6},{8,9},{9,8},{10,11... | collective-permute-start | bytes 24584 | tf_op jit(solution)/shard_map/ppermute | solution.py:416
  104.6 7.7 %collective-permute-start.19 = (f32[8,256]{1,0:T(8,128)S(1)}, f32[8,256]{1,0:T(8,128)S(1)}, u32[]{:S(2)}, u32[]{:S(2)}) collective-permute-start(f32[8,256]{1,0:T(8,128)S(1)} %pad_maximum_fusion.1.late_mine.mine), channel_id=1, source_target_pairs={{0,2},{1,3},{2,0},{3,1},{4,6},{5,7},{6,4},{7,5},{8,10},{9,11},{10,... | collective-permute-start | bytes 24584 | tf_op jit(solution)/shard_map/ppermute | solution.py:416
  (4 other events, 17.3 us)

commit v4 on v3

--- a/solution.py
+++ b/solution.py
@@ -213,10 +213,8 @@
     rows[...] = to_rows([None, None, total, squares])
 
 
-def forward1_kernel(low, high, fresh, gains, late_mine, late_other, mine, other, out, mean, rstd):
-    section = lax.axis_index("pipe")
-    first = section == 0
-    from_low = section <= lax.axis_size("pipe") // 2
+def forward1_kernel(arrived, fresh, gains, late_mine, late_other, mine, other, out, mean, rstd):
+    first = lax.axis_index("pipe") == 0
     width = out.shape[1]
     norm = [
         jnp.where(first, a, b)
@@ -224,7 +222,7 @@
     ]
 
     def pick(at):
-        return jnp.where(first, fresh[:, at], jnp.where(from_low, low[:, at], high[:, at]))
+        return jnp.where(first, fresh[:, at], arrived[:, at])
 
     forward_body(pick, gains, norm, out, mean, rstd)
 
@@ -490,7 +488,7 @@
     rows1_mine = join_gradients(rows1, over_tp(rows1, 1), width)
     sums1 = (rows1_mine, over_tp(rows1_mine, 2))
     fwd_out = forward(
-        forward1_kernel, "forward1", False, arrived, arrived, fresh_batch, gains, *sums1, *stats
+        forward1_kernel, "forward1", False, arrived, fresh_batch, gains, *sums1, *stats
     )[0]
     bwd_out = finish(finish1_kernel, "finish1", *tick1, *late_stats, gain_back, *sums1, last_grad)
     return (fwd_out[None], bwd_out[None], gain_total[None])

time: 119 us -> 119 us (level)
  no operation moved by 1% of the time
where the time goes in v4:
time: 119 us; the launch traced here: 118 us
  waiting for transfers between devices  46.6 us (39%)
  starting transfers between devices  41.7 us (35%)
  Pallas kernels  26.3 us (22%)
  local copies, waits for them, and re-layouts  1.8 us (2%)
    ppermute x11, starting transfers between devices, moved(): return lax.ppermute(value, 'pipe', pairs)  30.6 us
    ppermute x11, waiting for transfers between devices, moved(): return lax.ppermute(value, 'pipe', pairs)  25.6 us
    pallas_call x8, Pallas kernels, local_call(): pl.pallas_call(kernel, in_specs=[VMEM] * len(operands), out_specs=[VMEM]...  20.6 us
    ppermute x4, starting transfers between devices, over_tp(): return lax.ppermute(value, ('pipe', 'tp'), pairs)  10.8 us
    ppermute x4, waiting for transfers between devices, over_tp(): return lax.ppermute(value, ('pipe', 'tp'), pairs)  10.6 us
    ppermute x5, waiting for transfers between devices, over_tp(): return lax.ppermute(value, 'tp', [(i, i ^ mask) for i in range(PARTS)])  10.4 us
    pallas_call x1, Pallas kernels, pick(): pl.pallas_call(pick_kernel, in_specs=[SMEM, HBM, HBM, HBM, HBM], out_spec...  5.62 us
  transfers between devices with their start and end apart: 20, of which 9 were waited for; matrix products, arithmetic and copies ran while one was open for 1% of the time, Pallas kernels for 15%

profile of v4, /device:TPU:36, one launch (start us, length us, event | category | flops | bytes accessed | tf_op | source)
XLA Modules:
  0.0 118.2 jit_solution(2378213881493849781)
XLA Ops:
  0.7 5.6 %pick.1 = (bf16[256,1536]{1,0:T(8,128)(2,1)}, bf16[256,512]{1,0:T(8,128)(2,1)}, bf16[256,1024]{1,0:T(8,128)(2,1)}, bf16[256,1536]{1,0:T(8,128)(2,1)}, bf16[256,1536]{1,0:T(8,128)(2,1)}, /*index=5*/f32[16,256]{1,0:T(8,128)}) custom-call(s32[2,64]{1,0:T(2,128)} %plan.1, bf16[1,2,256,1536]{3,2,1,0:T(8,128)(2,1)} %kept.1, bf16[1,2,256,1536]{3,2,1,0:T(8,128)(2,1)} %own.1, ...), custom_call_target="tpu_custom_call" | custom-call | tf_op jit(solution)/shard_map/pick/pallas_call | solution.py:134
  6.4 1.4 %collective-permute-start.1 = (bf16[256,1024]{1,0:T(8,128)(2,1)}, bf16[256,1024]{1,0:T(8,128)(2,1)S(1)}, u32[]{:S(2)}, u32[]{:S(2)}) collective-permute-start(bf16[256,1024]{1,0:T(8,128)(2,1)} %get-tuple-element.29), channel_id=1, source_target_pairs={{252,12},{248,8},{244,4},{240,0},{236,28},{232,24},{228,20},{224,1... | collective-permute-start | bytes 1572872 | tf_op jit(solution)/shard_map/ppermute | solution.py:436
  9.3 2.0 %collective-permute-start = (f32[3,1536]{1,0:T(4,128)S(1)}, f32[3,1536]{1,0:T(4,128)S(1)}, u32[]{:S(2)}, u32[]{:S(2)}) collective-permute-start(f32[3,1536]{1,0:T(4,128)S(1)} %bitcast.12), channel_id=1, source_target_pairs={{0,124},{4,0},{8,4},{12,8},{16,12},{20,16},{24,20},{28,24},{32,28}... | collective-permute-start | bytes 55304 | tf_op jit(solution)/shard_map/ppermute | solution.py:436
  11.3 6.5 %collective-permute-start.7 = (bf16[256,1536]{1,0:T(8,128)(2,1)S(1)}, bf16[256,1536]{1,0:T(8,128)(2,1)S(1)}, u32[]{:S(2)}, u32[]{:S(2)}) collective-permute-start(bf16[256,1536]{1,0:T(8,128)(2,1)S(1)} %bitcast.9), channel_id=1, source_target_pairs={{0,124},{4,0},{8,4},{12,8},{16,12},{20,16},{24,20},{28,24},{32,28}... | collective-permute-start | bytes 2359304 | tf_op jit(solution)/shard_map/ppermute | solution.py:436
  17.8 6.4 %collective-permute-start.5 = (f32[16,256]{1,0:T(8,128)S(1)}, f32[16,256]{1,0:T(8,128)S(1)}, u32[]{:S(2)}, u32[]{:S(2)}) collective-permute-start(f32[16,256]{1,0:T(8,128)S(1)} %pad_maximum_fusion.mine.stats_mine), channel_id=1, source_target_pairs={{0,2},{1,3},{2,0},{3,1},{4,6},{5,7},{6,4},{7,5},{8,10},{9,11},{10,... | collective-permute-start | bytes 49160 | tf_op jit(solution)/shard_map/ppermute | solution.py:416
  24.2 1.3 %collective-permute-start.6 = (bf16[256,1536]{1,0:T(8,128)(2,1)}, bf16[256,1536]{1,0:T(8,128)(2,1)S(1)}, u32[]{:S(2)}, u32[]{:S(2)}) collective-permute-start(bf16[256,1536]{1,0:T(8,128)(2,1)} %get-tuple-element.36), channel_id=1, source_target_pairs={{252,124},{248,0},{244,4},{240,8},{236,12},{232,16},{228,20},{224,... | collective-permute-start | bytes 2359304 | tf_op jit(solution)/shard_map/ppermute | solution.py:436
  28.5 1.3 %collective-permute-start.8 = (f32[4,256]{1,0:T(4,128)S(1)}, f32[4,256]{1,0:T(4,128)S(1)}, u32[]{:S(2)}, u32[]{:S(2)}) collective-permute-start(f32[4,256]{1,0:T(4,128)S(1)} %pad_maximum_fusion.2), channel_id=1, source_target_pairs={{252,124},{248,0},{244,4},{240,8},{236,12},{232,16},{228,20},{224,... | collective-permute-start | bytes 12296 | tf_op jit(solution)/shard_map/ppermute | solution.py:436
  29.8 10.6 %collective-permute-done.5 = f32[16,256]{1,0:T(8,128)S(1)} collective-permute-done((f32[16,256]{1,0:T(8,128)S(1)}, f32[16,256]{1,0:T(8,128)S(1)}, u32[]{:S(2)}, u32[]{:S(2)}) %collective-permute-start.5) | collective-permute-done | bytes 16416 | tf_op jit(solution)/shard_map/ppermute | solution.py:416
  40.5 2.8 %forward0.1 = (bf16[256,1536]{1,0:T(8,128)(2,1)S(1)}, f32[8,256]{1,0:T(8,128)S(1)}) custom-call(bf16[256,1536]{1,0:T(8,128)(2,1)S(1)} %bitcast.8, f32[3,1536]{1,0:T(4,128)S(1)} %bitcast.14, f32[16,256]{1,0:T(8,128)S(1)} %pad_maximum_fusion.mine.stats_mine, f32[16,256]{1,0:T(8,128)S(1)} %add.46.other), custom_call_target="tpu_custom_call" | custom-call | tf_op jit(solution)/shard_map/forward0/pallas_call | solution.py:231
  43.3 4.2 %collective-permute-done.8.got_stats = f32[4,256]{1,0:T(4,128)S(1)} collective-permute-done((f32[4,256]{1,0:T(4,128)S(1)}, f32[4,256]{1,0:T(4,128)S(1)}, u32[]{:S(2)}, u32[]{:S(2)}) %collective-permute-start.8) | collective-permute-done | bytes 4128 | tf_op jit(solution)/shard_map/ppermute | solution.py:436
  48.3 4.2 %collective-permute-start.16 = (bf16[256,1024]{1,0:T(8,128)(2,1)S(1)}, bf16[256,1024]{1,0:T(8,128)(2,1)S(1)}, u32[]{:S(2)}, u32[]{:S(2)}) collective-permute-start(bf16[256,1024]{1,0:T(8,128)(2,1)S(1)} %collective-permute-done.1), channel_id=1, source_target_pairs={{12,0},{8,4},{4,8},{0,12},{28,16},{24,20},{20,24},{16,28},{44,32},... | collective-permute-start | bytes 1572872 | tf_op jit(solution)/shard_map/ppermute | solution.py:436
  52.5 1.3 %collective-permute-start.15 = (bf16[256,512]{1,0:T(8,128)(2,1)S(1)}, bf16[256,512]{1,0:T(8,128)(2,1)S(1)}, u32[]{:S(2)}, u32[]{:S(2)}) collective-permute-start(bf16[256,512]{1,0:T(8,128)(2,1)S(1)} %copy-done.7), channel_id=1, source_target_pairs={{252,0},{248,4},{244,8},{240,12},{236,16},{232,20},{228,24},{224,2... | collective-permute-start | bytes 786440 | tf_op jit(solution)/shard_map/ppermute | solution.py:436
  53.9 5.3 %early_backward0.1 = (f32[256,1536]{1,0:T(8,128)S(1)}, f32[4,1536]{1,0:T(4,128)S(1)}, f32[8,256]{1,0:T(8,128)S(1)}) custom-call(bf16[256,1536]{1,0:T(8,128)(2,1)S(1)} %collective-permute-done.6.z, bf16[256,1536]{1,0:T(8,128)(2,1)S(1)} %collective-permute-done.7.e, f32[3,1536]{1,0:T(4,128)S(1)} %collective-permute-done.gains, ...), custom_call_target="tpu_custom_call" | custom-call | tf_op jit(solution)/shard_map/early_backward0/pallas_call | solution.py:231
  59.1 1.9 %collective-permute-start.12 = (f32[4,1536]{1,0:T(4,128)S(1)}, f32[4,1536]{1,0:T(4,128)S(1)}, u32[]{:S(2)}, u32[]{:S(2)}) collective-permute-start(f32[4,1536]{1,0:T(4,128)S(1)} %get-tuple-element.42), channel_id=1, source_target_pairs={{0,4},{4,8},{8,12},{12,16},{16,20},{20,24},{24,28},{28,32},{32,36}... | collective-permute-start | bytes 73736 | tf_op jit(solution)/shard_map/ppermute | solution.py:436
  61.1 1.2 collective-permute-done.10
  62.3 3.1 %collective-permute-start.11 = (f32[8,256]{1,0:T(8,128)S(1)}, f32[8,256]{1,0:T(8,128)S(1)}, u32[]{:S(2)}, u32[]{:S(2)}) collective-permute-start(f32[8,256]{1,0:T(8,128)S(1)} %add.50.mine), channel_id=1, source_target_pairs={{0,2},{1,3},{2,0},{3,1},{4,6},{5,7},{6,4},{7,5},{8,10},{9,11},{10,... | collective-permute-start | bytes 24584 | tf_op jit(solution)/shard_map/ppermute | solution.py:416
  65.4 9.1 %collective-permute-done.12.got_part = f32[4,1536]{1,0:T(4,128)S(1)} collective-permute-done((f32[4,1536]{1,0:T(4,128)S(1)}, f32[4,1536]{1,0:T(4,128)S(1)}, u32[]{:S(2)}, u32[]{:S(2)}) %collective-permute-start.12) | collective-permute-done | bytes 24608 | tf_op jit(solution)/shard_map/ppermute | solution.py:436
  74.5 4.4 %collective-permute-start.13 = (f32[8,256]{1,0:T(8,128)S(1)}, f32[8,256]{1,0:T(8,128)S(1)}, u32[]{:S(2)}, u32[]{:S(2)}) collective-permute-start(f32[8,256]{1,0:T(8,128)S(1)} %get-tuple-element.44), channel_id=1, source_target_pairs={{0,4},{4,8},{8,12},{12,16},{16,20},{20,24},{24,28},{28,32},{32,36}... | collective-permute-start | bytes 24584 | tf_op jit(solution)/shard_map/ppermute | solution.py:436
  80.2 5.5 %collective-permute-start.14 = (bf16[256,1536]{1,0:T(8,128)(2,1)S(1)}, bf16[256,1536]{1,0:T(8,128)(2,1)S(1)}, u32[]{:S(2)}, u32[]{:S(2)}) collective-permute-start(bf16[256,1536]{1,0:T(8,128)(2,1)S(1)} %get-tuple-element.45), channel_id=1, source_target_pairs={{0,4},{4,8},{8,12},{12,16},{16,20},{20,24},{24,28},{28,32},{32,36}... | collective-permute-start | bytes 2359304 | tf_op jit(solution)/shard_map/ppermute | solution.py:436
  85.7 12.1 %collective-permute-done.15.dz = bf16[256,512]{1,0:T(8,128)(2,1)S(1)} collective-permute-done((bf16[256,512]{1,0:T(8,128)(2,1)S(1)}, bf16[256,512]{1,0:T(8,128)(2,1)S(1)}, u32[]{:S(2)}, u32[]{:S(2)}) %collective-permute-start.15) | collective-permute-done | bytes 262176 | tf_op jit(solution)/shard_map/ppermute | solution.py:436
  97.8 5.5 %backward1.1 = (f32[256,1536]{1,0:T(8,128)S(1)}, f32[3,1536]{1,0:T(4,128)S(1)}, f32[8,256]{1,0:T(8,128)S(1)}) custom-call(bf16[256,1536]{1,0:T(8,128)(2,1)S(1)} %copy-done.3, bf16[256,512]{1,0:T(8,128)(2,1)S(1)} %collective-permute-done.15.dz, bf16[256,1024]{1,0:T(8,128)(2,1)S(1)} %collective-permute-done.16.az, bf16[256,1536]{1,0:T(8,128)(2,1)S(1)} %early_finish0.1.oe, ...), custom_call_target="tpu_custom_call" | custom-call | tf_op jit(solution)/shard_map/backward1/pallas_call | solution.py:231
  105.3 6.9 %collective-permute-done.19.late_other.other = f32[8,256]{1,0:T(8,128)S(1)} collective-permute-done((f32[8,256]{1,0:T(8,128)S(1)}, f32[8,256]{1,0:T(8,128)S(1)}, u32[]{:S(2)}, u32[]{:S(2)}) %collective-permute-start.19) | collective-permute-done | bytes 8224 | tf_op jit(solution)/shard_map/ppermute | solution.py:414
  112.3 2.5 %finish1.1 = bf16[256,1536]{1,0:T(8,128)(2,1)} custom-call(bf16[256,1536]{1,0:T(8,128)(2,1)S(1)} %copy-done.3, bf16[256,512]{1,0:T(8,128)(2,1)S(1)} %collective-permute-done.15.dz, bf16[256,1024]{1,0:T(8,128)(2,1)S(1)} %collective-permute-done.16.az, bf16[256,1536]{1,0:T(8,128)(2,1)S(1)} %early_finish0.1.oe, ...), custom_call_target="tpu_custom_call" | custom-call | tf_op jit(solution)/shard_map/finish1/pallas_call | solution.py:231
  114.8 3.4 %forward1.1 = bf16[256,1536]{1,0:T(8,128)(2,1)} custom-call(bf16[256,1536]{1,0:T(8,128)(2,1)S(1)} %collective-permute-done.14.arrived, bf16[256,1536]{1,0:T(8,128)(2,1)S(1)} %copy-done.1, f32[3,1536]{1,0:T(4,128)S(1)} %bitcast.16, f32[8,256]{1,0:T(8,128)S(1)} %pad_maximum_fusion.1.late_mine.mine, f32[8,256]{1,0:T(8,128)S(1)} %collective-permute-done.19.late_other.other, ...), custom_call_target="tpu_custom_call" | custom-call | tf_op jit(solution)/shard_map/forward1/pallas_call | solution.py:231
  (56 shorter events, 8.7 us)
Async XLA Ops:
  0.6 10.6 %copy-start.4 = (bf16[1,256,1536]{2,1,0:T(8,128)(2,1)S(1)}, bf16[1,256,1536]{2,1,0:T(8,128)(2,1)}, u32[]{:S(2)}) copy-start(bf16[1,256,1536]{2,1,0:T(8,128)(2,1)} %param.9) | copy-start | bytes 2359300
  6.3 34.2 %copy-start = (bf16[1,256,1536]{2,1,0:T(8,128)(2,1)S(1)}, bf16[1,256,1536]{2,1,0:T(8,128)(2,1)}, u32[]{:S(2)}) copy-start(bf16[1,256,1536]{2,1,0:T(8,128)(2,1)} %stream.1) | copy-start | bytes 2359300
  6.3 1.5 %collective-permute-start.2 = (f32[16,256]{1,0:T(8,128)}, f32[16,256]{1,0:T(8,128)S(1)}, u32[]{:S(2)}, u32[]{:S(2)}) collective-permute-start(f32[16,256]{1,0:T(8,128)} %get-tuple-element.31), channel_id=1, source_target_pairs={{0,1},{1,0},{2,3},{3,2},{4,5},{5,4},{6,7},{7,6},{8,9},{9,8},{10,11... | collective-permute-start | bytes 49160 | tf_op jit(solution)/shard_map/ppermute | solution.py:414
  6.4 19.2 %collective-permute-start.1 = (bf16[256,1024]{1,0:T(8,128)(2,1)}, bf16[256,1024]{1,0:T(8,128)(2,1)S(1)}, u32[]{:S(2)}, u32[]{:S(2)}) collective-permute-start(bf16[256,1024]{1,0:T(8,128)(2,1)} %get-tuple-element.29), channel_id=1, source_target_pairs={{252,12},{248,8},{244,4},{240,0},{236,28},{232,24},{228,20},{224,1... | collective-permute-start | bytes 1572872 | tf_op jit(solution)/shard_map/ppermute | solution.py:436
  8.6 15.7 %collective-permute-start.3 = (f32[16,256]{1,0:T(8,128)S(1)}, f32[16,256]{1,0:T(8,128)S(1)}, u32[]{:S(2)}, u32[]{:S(2)}) collective-permute-start(f32[16,256]{1,0:T(8,128)S(1)} %pad_maximum_fusion.mine.stats_mine), channel_id=1, source_target_pairs={{128,130},{129,131},{130,128},{131,129},{132,134},{133,135},{134,1... | collective-permute-start | bytes 49160 | tf_op jit(solution)/shard_map/ppermute | solution.py:416
  9.3 16.3 %collective-permute-start = (f32[3,1536]{1,0:T(4,128)S(1)}, f32[3,1536]{1,0:T(4,128)S(1)}, u32[]{:S(2)}, u32[]{:S(2)}) collective-permute-start(f32[3,1536]{1,0:T(4,128)S(1)} %bitcast.12), channel_id=1, source_target_pairs={{0,124},{4,0},{8,4},{12,8},{16,12},{20,16},{24,20},{28,24},{32,28}... | collective-permute-start | bytes 55304 | tf_op jit(solution)/shard_map/ppermute | solution.py:436
  11.3 42.5 %collective-permute-start.7 = (bf16[256,1536]{1,0:T(8,128)(2,1)S(1)}, bf16[256,1536]{1,0:T(8,128)(2,1)S(1)}, u32[]{:S(2)}, u32[]{:S(2)}) collective-permute-start(bf16[256,1536]{1,0:T(8,128)(2,1)S(1)} %bitcast.9), channel_id=1, source_target_pairs={{0,124},{4,0},{8,4},{12,8},{16,12},{20,16},{24,20},{28,24},{32,28}... | collective-permute-start | bytes 2359304 | tf_op jit(solution)/shard_map/ppermute | solution.py:436
  17.8 22.7 %collective-permute-start.5 = (f32[16,256]{1,0:T(8,128)S(1)}, f32[16,256]{1,0:T(8,128)S(1)}, u32[]{:S(2)}, u32[]{:S(2)}) collective-permute-start(f32[16,256]{1,0:T(8,128)S(1)} %pad_maximum_fusion.mine.stats_mine), channel_id=1, source_target_pairs={{0,2},{1,3},{2,0},{3,1},{4,6},{5,7},{6,4},{7,5},{8,10},{9,11},{10,... | collective-permute-start | bytes 49160 | tf_op jit(solution)/shard_map/ppermute | solution.py:416
  24.2 29.6 %collective-permute-start.6 = (bf16[256,1536]{1,0:T(8,128)(2,1)}, bf16[256,1536]{1,0:T(8,128)(2,1)S(1)}, u32[]{:S(2)}, u32[]{:S(2)}) collective-permute-start(bf16[256,1536]{1,0:T(8,128)(2,1)} %get-tuple-element.36), channel_id=1, source_target_pairs={{252,124},{248,0},{244,4},{240,8},{236,12},{232,16},{228,20},{224,... | collective-permute-start | bytes 2359304 | tf_op jit(solution)/shard_map/ppermute | solution.py:436
  26.7 1.2 collective-permute-start.4
  27.9 19.6 %collective-permute-start.9 = (f32[8,256]{1,0:T(8,128)S(1)}, f32[8,256]{1,0:T(8,128)S(1)}, u32[]{:S(2)}, u32[]{:S(2)}) collective-permute-start(f32[8,256]{1,0:T(8,128)S(1)} %add.45.mine), channel_id=1, source_target_pairs={{128,130},{129,131},{130,128},{131,129},{132,134},{133,135},{134,1... | collective-permute-start | bytes 24584 | tf_op jit(solution)/shard_map/ppermute | solution.py:416
  28.5 18.9 %collective-permute-start.8 = (f32[4,256]{1,0:T(4,128)S(1)}, f32[4,256]{1,0:T(4,128)S(1)}, u32[]{:S(2)}, u32[]{:S(2)}) collective-permute-start(f32[4,256]{1,0:T(4,128)S(1)} %pad_maximum_fusion.2), channel_id=1, source_target_pairs={{252,124},{248,0},{244,4},{240,8},{236,12},{232,16},{228,20},{224,... | collective-permute-start | bytes 12296 | tf_op jit(solution)/shard_map/ppermute | solution.py:436
  47.5 50.3 %collective-permute-start.17 = (bf16[256,1536]{1,0:T(8,128)(2,1)S(1)}, bf16[256,1536]{1,0:T(8,128)(2,1)S(1)}, u32[]{:S(2)}, u32[]{:S(2)}) collective-permute-start(bf16[256,1536]{1,0:T(8,128)(2,1)S(1)} %late_finish0.1), channel_id=1, source_target_pairs={{128,124},{132,128},{136,132},{140,136},{144,140},{148,144},{152,1... | collective-permute-start | bytes 2359304 | tf_op jit(solution)/shard_map/ppermute | solution.py:436
  48.3 49.5 %collective-permute-start.16 = (bf16[256,1024]{1,0:T(8,128)(2,1)S(1)}, bf16[256,1024]{1,0:T(8,128)(2,1)S(1)}, u32[]{:S(2)}, u32[]{:S(2)}) collective-permute-start(bf16[256,1024]{1,0:T(8,128)(2,1)S(1)} %collective-permute-done.1), channel_id=1, source_target_pairs={{12,0},{8,4},{4,8},{0,12},{28,16},{24,20},{20,24},{16,28},{44,32},... | collective-permute-start | bytes 1572872 | tf_op jit(solution)/shard_map/ppermute | solution.py:436
  52.5 45.3 %collective-permute-start.15 = (bf16[256,512]{1,0:T(8,128)(2,1)S(1)}, bf16[256,512]{1,0:T(8,128)(2,1)S(1)}, u32[]{:S(2)}, u32[]{:S(2)}) collective-permute-start(bf16[256,512]{1,0:T(8,128)(2,1)S(1)} %copy-done.7), channel_id=1, source_target_pairs={{252,0},{248,4},{244,8},{240,12},{236,16},{232,20},{228,24},{224,2... | collective-permute-start | bytes 786440 | tf_op jit(solution)/shard_map/ppermute | solution.py:436
  59.1 15.4 %collective-permute-start.12 = (f32[4,1536]{1,0:T(4,128)S(1)}, f32[4,1536]{1,0:T(4,128)S(1)}, u32[]{:S(2)}, u32[]{:S(2)}) collective-permute-start(f32[4,1536]{1,0:T(4,128)S(1)} %get-tuple-element.42), channel_id=1, source_target_pairs={{0,4},{4,8},{8,12},{12,16},{16,20},{20,24},{24,28},{28,32},{32,36}... | collective-permute-start | bytes 73736 | tf_op jit(solution)/shard_map/ppermute | solution.py:436
  61.0 1.3 %collective-permute-start.10 = (f32[8,256]{1,0:T(8,128)S(1)}, f32[8,256]{1,0:T(8,128)S(1)}, u32[]{:S(2)}, u32[]{:S(2)}) collective-permute-start(f32[8,256]{1,0:T(8,128)S(1)} %get-tuple-element.40), channel_id=1, source_target_pairs={{0,1},{1,0},{2,3},{3,2},{4,5},{5,4},{6,7},{7,6},{8,9},{9,8},{10,11... | collective-permute-start | bytes 24584 | tf_op jit(solution)/shard_map/ppermute | solution.py:414
  62.3 16.6 %collective-permute-start.11 = (f32[8,256]{1,0:T(8,128)S(1)}, f32[8,256]{1,0:T(8,128)S(1)}, u32[]{:S(2)}, u32[]{:S(2)}) collective-permute-start(f32[8,256]{1,0:T(8,128)S(1)} %add.50.mine), channel_id=1, source_target_pairs={{0,2},{1,3},{2,0},{3,1},{4,6},{5,7},{6,4},{7,5},{8,10},{9,11},{10,... | collective-permute-start | bytes 24584 | tf_op jit(solution)/shard_map/ppermute | solution.py:416
  74.5 5.7 %collective-permute-start.13 = (f32[8,256]{1,0:T(8,128)S(1)}, f32[8,256]{1,0:T(8,128)S(1)}, u32[]{:S(2)}, u32[]{:S(2)}) collective-permute-start(f32[8,256]{1,0:T(8,128)S(1)} %get-tuple-element.44), channel_id=1, source_target_pairs={{0,4},{4,8},{8,12},{12,16},{16,20},{20,24},{24,28},{28,32},{32,36}... | collective-permute-start | bytes 24584 | tf_op jit(solution)/shard_map/ppermute | solution.py:436
  78.9 19.0 %copy-start.2 = (bf16[256,1536]{1,0:T(8,128)(2,1)S(1)}, bf16[256,1536]{1,0:T(8,128)(2,1)}, u32[]{:S(2)}) copy-start(bf16[256,1536]{1,0:T(8,128)(2,1)} %le.3) | copy-start | bytes 2359300
  78.9 19.0 %copy-start.3 = (bf16[256,1536]{1,0:T(8,128)(2,1)S(1)}, bf16[256,1536]{1,0:T(8,128)(2,1)}, u32[]{:S(2)}) copy-start(bf16[256,1536]{1,0:T(8,128)(2,1)} %get-tuple-element.46.oz) | copy-start | bytes 2359300
  80.2 34.6 %collective-permute-start.14 = (bf16[256,1536]{1,0:T(8,128)(2,1)S(1)}, bf16[256,1536]{1,0:T(8,128)(2,1)S(1)}, u32[]{:S(2)}, u32[]{:S(2)}) collective-permute-start(bf16[256,1536]{1,0:T(8,128)(2,1)S(1)} %get-tuple-element.45), channel_id=1, source_target_pairs={{0,4},{4,8},{8,12},{12,16},{16,20},{20,24},{24,28},{28,32},{32,36}... | collective-permute-start | bytes 2359304 | tf_op jit(solution)/shard_map/ppermute | solution.py:436
  103.3 1.2 %collective-permute-start.18 = (f32[8,256]{1,0:T(8,128)S(1)}, f32[8,256]{1,0:T(8,128)S(1)}, u32[]{:S(2)}, u32[]{:S(2)}) collective-permute-start(f32[8,256]{1,0:T(8,128)S(1)} %add.51), channel_id=1, source_target_pairs={{0,1},{1,0},{2,3},{3,2},{4,5},{5,4},{6,7},{7,6},{8,9},{9,8},{10,11... | collective-permute-start | bytes 24584 | tf_op jit(solution)/shard_map/ppermute | solution.py:414
  104.6 7.6 %collective-permute-start.19 = (f32[8,256]{1,0:T(8,128)S(1)}, f32[8,256]{1,0:T(8,128)S(1)}, u32[]{:S(2)}, u32[]{:S(2)}) collective-permute-start(f32[8,256]{1,0:T(8,128)S(1)} %pad_maximum_fusion.1.late_mine.mine), channel_id=1, source_target_pairs={{0,2},{1,3},{2,0},{3,1},{4,6},{5,7},{6,4},{7,5},{8,10},{9,11},{10,... | collective-permute-start | bytes 24584 | tf_op jit(solution)/shard_map/ppermute | solution.py:414
  (4 other events, 17.3 us)
